TPU v7x, 128 devices: a whole 4x4x4 slice. The times are simulated.
128 devices in a mesh: depth: 4 (over y_hi, core), row: 4 (over x), col: 8 (over z, y_lo).
Axes of the slice: x: 4, y: 4 (y_hi: 2, y_lo: 2; y = y_hi * 2 + y_lo), z: 4, core: 2. Of those that a mesh axis runs over, the one named last changes fastest.
Arguments:
- inputs: bfloat16 [1024, 6144], P(('depth', 'col'), 'row'), may hold values from -6 to 6
- in_weight: bfloat16 [6144, 24576], P(('row', 'depth'), 'col'), may hold values from -0.078125 to 0.078125
- out_weight: bfloat16 [24576, 6144], P(('col', 'depth'), 'row'), may hold values from -0.0390625 to 0.0390625
- out_grad: bfloat16 [1024, 6144], P(('depth', 'col'), 'row'), may hold values from -6 to 6
Outputs:
- mixed: bfloat16 [1024, 6144], P(('depth', 'col'), 'row')
- grad_in: bfloat16 [1024, 6144], P(('depth', 'col'), 'row')
- grad_w_in: bfloat16 [6144, 24576], P(('row', 'depth'), 'col')
- grad_w_out: bfloat16 [24576, 6144], P(('col', 'depth'), 'row')
All inputs are finite; a program needn't handle non-finite values.
Results may differ from a plain program's by a relative error of at most 0.025.
Values may be sent and summed in bfloat16 or wider, within the bound.
No kernel may reach another device: no remote copies, remote signals or barrier semaphores. Data moves between devices by JAX's collectives and lax.ppermute only.
A program may use at most 128 MiB of HBM per device.

v0:
```python
import math

import jax
import jax.numpy as jnp
from jax import lax
from jax.experimental import pallas as pl
from jax.experimental.pallas import tpu as pltpu
from jax.sharding import Mesh, PartitionSpec as P

GELU_SCALE = math.sqrt(2.0 / math.pi)
CUBIC = 0.044715
BACK_DIMS = (((1,), (1,)), ((), ()))
LEAD_DIMS = (((0,), (0,)), ((), ()))
PLAIN_DIMS = (((1,), (0,)), ((), ()))
AXES = ("b", "c", "x", "z", "a")
BF16, F32 = jnp.bfloat16, jnp.float32
ANY = pl.BlockSpec(memory_space=pl.ANY)
SMEM = pl.BlockSpec(memory_space=pltpu.SMEM)
WHOLE = pl.BlockSpec(memory_space=pltpu.VMEM)
SMALL = pl.CostEstimate(flops=1024, bytes_accessed=1024, transcendentals=0)


def place(x, y, z, c):
    b, a = divmod(y % 4, 2)
    return (((b * 2 + c) * 4 + x % 4) * 4 + z % 4) * 2 + a


def shift(value, dx=0, dy=0, dz=0, fc=0):
    pairs = [
        (place(x, y, z, c), place(x + dx, y + dy, z + dz, c ^ fc))
        for x in range(4)
        for y in range(4)
        for z in range(4)
        for c in range(2)
    ]
    return lax.ppermute(value, AXES, pairs)


def mul(left, right, dims):
    return lax.dot_general(left, right, dims, preferred_element_type=F32).astype(BF16)


def gelu_both(value):
    inner = GELU_SCALE * (value + CUBIC * value * value * value)
    tanh_value = jnp.tanh(inner)
    slope = 0.5 * (1.0 + tanh_value) + 0.5 * value * (1.0 - tanh_value * tanh_value) * GELU_SCALE * (
        1.0 + 3.0 * CUBIC * value * value
    )
    return 0.5 * value * (1.0 + tanh_value), slope


def at(blocks, index):
    return lax.dynamic_index_in_dim(blocks, index, 0, keepdims=False)


def after(value, *others):
    return lax.optimization_barrier((value,) + others)[0]


def call(kernel, name, outs, operands, specs=None, scratch=(), after=(), vmem=12, grid=(), out_specs=None):
    n, m = len(operands), len(after)

    def waiting(*refs):
        kernel(*refs[:n], *refs[n + m :])

    return pl.pallas_call(
        waiting,
        grid=grid,
        out_shape=[jax.ShapeDtypeStruct(shape, BF16) for shape in outs],
        in_specs=list(specs or [ANY] * n) + [ANY] * m,
        out_specs=out_specs or [WHOLE] * len(outs),
        scratch_shapes=list(scratch),
        compiler_params=pltpu.CompilerParams(vmem_limit_bytes=vmem * 1024 * 1024),
        cost_estimate=SMALL,
        name=name,
    )(*operands, *after)


def numbers_of(numbers):
    return jnp.stack([jnp.int32(number) for number in numbers])


def start(copies):
    for copy in copies:
        copy.start()
    return copies


def finish(copies):
    for copy in copies:
        copy.wait()


def spread(blocks, after):
    def kernel(*refs):
        outs, sems = refs[4:6], refs[6]
        finish(
            start(
                [
                    pltpu.make_async_copy(refs[i].at[pl.ds(h * 32, 32)], outs[h].at[pl.ds(i * 32, 32)], sems.at[i, h])
                    for i in range(4)
                    for h in range(2)
                ]
            )
        )

    return call(kernel, "spread", [(128, 1536)] * 2, blocks, None, [pltpu.SemaphoreType.DMA((4, 2))], after, 4)


def held(rows, after):
    def kernel(rows_ref, out_ref, sem):
        finish(start([pltpu.make_async_copy(rows_ref, out_ref, sem.at[0])]))

    return call(kernel, "held", [rows.shape], [rows], None, [pltpu.SemaphoreType.DMA((1,))], after, 4)[0]


def copied(shape, parts, after=()):
    n = len(parts)

    def kernel(numbers, *refs):
        out, sems = refs[n], refs[n + 1]
        copies = []
        for i in range(n):
            rows = refs[i].shape[0]
            col, row, out_col = (numbers[3 * i + k] for k in range(3))
            source = refs[i].at[:, pl.ds(pl.multiple_of(col * 1536, 1536), 1536)]
            target = out.at[pl.ds(pl.multiple_of(row * rows, rows), rows), pl.ds(pl.multiple_of(out_col * 1536, 1536), 1536)]
            copies.append(pltpu.make_async_copy(source, target, sems.at[i]))
        finish(start(copies))

    return call(
        kernel,
        "copied",
        [shape],
        [numbers_of([v for part in parts for v in part[1:]]), *[part[0] for part in parts]],
        [SMEM] + [ANY] * n,
        [pltpu.SemaphoreType.DMA((n,))],
        after,
        6,
    )[0]


def last(terms, after):
    def kernel(*refs):
        result = total([ref[...] for ref in refs[:4]]).astype(BF16)
        refs[4][...], refs[5][...] = result[:32], result[32:]

    return call(kernel, "last", [(32, 1536)] * 2, terms, [WHOLE] * 4, (), after, 4)


def put(parts, split=1):
    blocks = [block for _, block in parts]
    n, rows, width = len(parts), blocks[0].shape[0] // split, blocks[0].shape[1]

    def kernel(index_ref, *refs):
        outs, sems = refs[n : n + split], refs[n + split]
        copies = [
            pltpu.make_async_copy(
                refs[i].at[pl.ds(h * rows, rows)],
                outs[h].at[pl.ds(pl.multiple_of(index_ref[i] * rows, rows), rows)],
                sems.at[i, h],
            )
            for i in range(n)
            for h in range(split)
        ]
        for copy in copies:
            copy.start()
        for copy in copies:
            copy.wait()

    return pl.pallas_call(
        kernel,
        out_shape=[jax.ShapeDtypeStruct((n * rows, width), BF16)] * split,
        in_specs=[pl.BlockSpec(memory_space=pltpu.SMEM)] + [pl.BlockSpec(memory_space=pl.ANY)] * n,
        out_specs=[pl.BlockSpec(memory_space=pltpu.VMEM)] * split,
        scratch_shapes=[pltpu.SemaphoreType.DMA((n, split))],
        compiler_params=pltpu.CompilerParams(vmem_limit_bytes=10 * 1024 * 1024),
        name="put",
    )(jnp.stack([jnp.int32(index) for index, _ in parts]), *blocks)


def product(blocks, places, weight, dims, keep=False, joined=False, after=(), first=(0,) * 4):
    wide, back = 512, dims == BACK_DIMS
    n, m = len(blocks), len(after)
    n_out = 1 if joined else n
    rows = 512 // n_out

    def kernel(place_ref, *refs):
        w_ref, refs_after = refs[n], refs[n + 1 + m :]
        outs, rest = refs_after[:n_out], refs_after[n_out:]
        whole, sems = rest[0], rest[1]

        @pl.when(pl.program_id(0) == 0)
        def _():
            copies = [
                pltpu.make_async_copy(
                    refs[i].at[pl.ds(first[i], 128)],
                    whole.at[pl.ds(pl.multiple_of(place_ref[i] * 128, 128), 128)],
                    sems.at[i],
                )
                for i in range(n)
            ]
            for copy in copies:
                copy.start()
            for copy in copies:
                copy.wait()

        result = lax.dot_general(whole[...], w_ref[...], dims, preferred_element_type=F32).astype(BF16)
        for i in range(n_out):
            outs[i][...] = result[i * rows : (i + 1) * rows]

    w_block = ((wide, 1536), lambda t: (t, 0)) if back else ((1536, wide), lambda t: (0, t))
    out_shape = [jax.ShapeDtypeStruct((rows, 1536), BF16)] * n_out
    out_specs = [pl.BlockSpec((rows, wide), lambda t: (0, t))] * n_out
    scratch = [pltpu.VMEM((512, 1536), BF16), pltpu.SemaphoreType.DMA((n,))]
    if keep:
        out_shape.append(jax.ShapeDtypeStruct((512, 1536), BF16))
        out_specs.append(pl.BlockSpec((512, 1536), lambda t: (0, 0)))
        scratch = scratch[1:]
    return pl.pallas_call(
        kernel,
        grid=(1536 // wide,),
        out_shape=out_shape,
        in_specs=[pl.BlockSpec(memory_space=pltpu.SMEM)]
        + [pl.BlockSpec(memory_space=pl.ANY)] * n
        + [pl.BlockSpec(*w_block)]
        + [pl.BlockSpec(memory_space=pl.ANY)] * m,
        out_specs=out_specs,
        scratch_shapes=scratch,
        compiler_params=pltpu.CompilerParams(vmem_limit_bytes=16 * 1024 * 1024),
        cost_estimate=pl.CostEstimate(flops=2 * 512 * 1536 * 1536, bytes_accessed=8 << 20, transcendentals=0),
        name="product",
    )(jnp.stack([jnp.int32(place) for place in places]), *blocks, weight, *after)


def total(parts):
    result = parts[0].astype(F32)
    for part in parts[1:]:
        result = result + part.astype(F32)
    return result


def summed(rows, me, axis):
    blocks = rows.reshape(4, rows.shape[0] // 4, rows.shape[1])
    return total([at(blocks, me)] + [shift(at(blocks, (me + i) % 4), **{axis: i}) for i in (1, 2, 3)])


def scatter(parts, axis):
    return [parts[0]] + [shift(parts[i], **{axis: i}) for i in (1, 2, 3)]


def gather(block, axis):
    return [block] + [shift(block, **{axis: -i}) for i in (1, 2, 3)]


def body(inputs, in_weight, out_weight, out_grad):
    b, c, x, z = (lax.axis_index(name) for name in ("b", "c", "x", "z"))
    units = 1536
    quarters = (0, 128, 256, 384)
    in_z = [(x + i) % 4 for i in range(4)]
    to_x = [(z + i - x) % 4 for i in range(4)]
    to_z = [(x + i - z) % 4 for i in range(4)]

    out_other = shift(out_weight, fc=1)
    own = lax.dynamic_slice(in_weight, (0, b * units), (384, units))
    own_other = shift(own, fc=1)
    both = gather(jnp.concatenate([out_grad, inputs]), "dy")
    grad_128, tok_128 = spread(both, [out_other])
    grad_blocks = gather(grad_128, "dz")
    away = shift(after(lax.dynamic_slice(in_weight, (0, (1 - b) * units), (384, units)), grad_128), dy=2)

    (out_tile,) = put([(c, out_weight), (1 - c, out_other)])
    grad_parts = product(grad_blocks, to_x, out_tile, BACK_DIMS)
    grad_act = total(scatter(grad_parts, "dx"))

    tok_rows = lax.all_gather(after(tok_128, *grad_blocks), "z", axis=0, tiled=True)
    away = after(away, grad_parts[0])
    (in_tile,) = put(
        [
            (2 * b + c, own),
            (2 * (1 - b) + c, away),
            (2 * b + 1 - c, own_other),
            (2 * (1 - b) + 1 - c, shift(away, fc=1)),
        ]
    )
    preact = summed(mul(tok_rows, in_tile, PLAIN_DIMS), x, "dx")
    act, slope = gelu_both(preact)
    pre_blocks = gather((grad_act * slope).astype(BF16), "dx")
    act_blocks = gather(after(act.astype(BF16), *pre_blocks), "dx")

    (grad_pre,) = put(list(zip(in_z, pre_blocks)))

    def columns(which):
        return jnp.concatenate(
            [lax.dynamic_slice(tok_rows, (0, (2 * i + which) * 384), (512, 384)) for i in range(2)], axis=1
        )

    tok_mine, tok_other = columns(c), columns(1 - c)

    other = shift(mul(tok_other, grad_pre, LEAD_DIMS), fc=1)
    in_part = mul(grad_pre, in_tile, BACK_DIMS)
    other, in_part = lax.optimization_barrier((other, in_part))
    in_rows = lax.psum_scatter(in_part, "z", scatter_dimension=0, tiled=True)
    rows = total([mul(tok_mine, grad_pre, LEAD_DIMS), other]).astype(BF16).reshape(2, 384, units)
    kept, sent = at(rows, b), at(rows, 1 - b)
    arrived = shift(sent, dy=2)
    act_blocks[0] = after(act_blocks[0], sent)
    (act_rows,) = put(list(zip(in_z, act_blocks)))
    (grad_rows,) = put([((z + i) % 4, grad_blocks[i]) for i in range(4)])
    out_rows = summed(mul(act_rows, out_tile, PLAIN_DIMS), z, "dz").astype(BF16)
    grad_w_out = lax.psum_scatter(mul(act_rows, grad_rows, LEAD_DIMS), "c", scatter_dimension=0, tiled=True)
    out_rows, arrived = lax.optimization_barrier((out_rows, arrived))
    grad_w_in = copied((384, 2 * units), [(kept, 0, 0, b), (arrived, 0, 0, 1 - b)])
    parts = [jnp.concatenate([v[i * 32 : (i + 1) * 32] for v in (out_rows, in_rows)]) for i in range(4)]
    return (*last(scatter(parts, "dy"), [grad_w_in]), grad_w_in, grad_w_out)


def solution(mesh):
    fine = Mesh(mesh.devices.reshape(2, 2, 4, 4, 2), AXES)
    tokens = P(("b", "c", "z", "a"), "x")
    w_in = P(("x", "b", "c"), ("z", "a"))
    w_out = P(("z", "a", "b", "c"), "x")
    return jax.shard_map(
        body,
        mesh=fine,
        in_specs=(tokens, w_in, w_out, tokens),
        out_specs=(tokens, tokens, w_in, w_out),
        check_vma=False,
    )
```

profile of v0, /device:TPU:1, one launch (start us, length us, event | category | flops | bytes accessed | tf_op | source)
XLA Modules:
  0.0 224.0 jit_solution(921779266056239080)
XLA Ops:
  10.5 2.8 %collective-permute-start = (bf16[64,1536]{1,0:T(8,128)(2,1)S(1)}, bf16[64,1536]{1,0:T(8,128)(2,1)S(1)}, u32[]{:S(2)}, u32[]{:S(2)}) collective-permute-start(bf16[64,1536]{1,0:T(8,128)(2,1)S(1)} %constant_dynamic-update-slice_fusion.refs_0_), channel_id=1, source_target_pairs={{0,65},{32,97},{2,67},{34,99},{4,69},{36,101},{6,71},{38,103},{1,0... | collective-permute-start | bytes 589832 | tf_op jit(solution)/shard_map/ppermute | solution.py:36
  14.4 7.3 %collective-permute-done.refs_1_ = bf16[64,1536]{1,0:T(8,128)(2,1)S(1)} collective-permute-done((bf16[64,1536]{1,0:T(8,128)(2,1)S(1)}, bf16[64,1536]{1,0:T(8,128)(2,1)S(1)}, u32[]{:S(2)}, u32[]{:S(2)}) %collective-permute-start) | collective-permute-done | bytes 196640 | tf_op jit(solution)/shard_map/ppermute | solution.py:36
  21.7 4.1 %collective-permute-done.2.refs_3_ = bf16[64,1536]{1,0:T(8,128)(2,1)S(1)} collective-permute-done((bf16[64,1536]{1,0:T(8,128)(2,1)S(1)}, bf16[64,1536]{1,0:T(8,128)(2,1)S(1)}, u32[]{:S(2)}, u32[]{:S(2)}) %collective-permute-start.2) | collective-permute-done | bytes 196640 | tf_op jit(solution)/shard_map/ppermute | solution.py:36
  28.4 3.8 %collective-permute-start.4 = (bf16[128,1536]{1,0:T(8,128)(2,1)}, bf16[128,1536]{1,0:T(8,128)(2,1)}, u32[]{:S(2)}, u32[]{:S(2)}) collective-permute-start(bf16[128,1536]{1,0:T(8,128)(2,1)} %get-tuple-element.22.refs_0_), channel_id=1, source_target_pairs={{0,6},{32,38},{2,0},{34,32},{4,2},{36,34},{6,4},{38,36},{1,7},{33,... | collective-permute-start | bytes 1179656 | tf_op jit(solution)/shard_map/ppermute | solution.py:36
  32.9 2.8 %constant_dynamic-slice_fusion.4 = (bf16[384,1536]{1,0:T(8,128)(2,1)}, bf16[384,1536]{1,0:T(8,128)(2,1)S(1)}) fusion(bf16[384,3072]{1,0:T(8,128)(2,1)} %param.5, s32[]{:T(128)S(6)} %select_n.118, s32[]{:T(128)S(6)} %select_n.117), kind=kLoop, calls=%fused_computation.48 | loop fusion | bytes 4718600 | tf_op jit(solution)/shard_map/dynamic_slice | solution.py:270
  36.0 12.7 %collective-permute-done.4.refs_1_ = bf16[128,1536]{1,0:T(8,128)(2,1)} collective-permute-done((bf16[128,1536]{1,0:T(8,128)(2,1)}, bf16[128,1536]{1,0:T(8,128)(2,1)}, u32[]{:S(2)}, u32[]{:S(2)}) %collective-permute-start.4) | collective-permute-done | bytes 393248 | tf_op jit(solution)/shard_map/ppermute | solution.py:36
  48.8 4.1 %collective-permute-done.6.refs_3_ = bf16[128,1536]{1,0:T(8,128)(2,1)} collective-permute-done((bf16[128,1536]{1,0:T(8,128)(2,1)}, bf16[128,1536]{1,0:T(8,128)(2,1)}, u32[]{:S(2)}, u32[]{:S(2)}) %collective-permute-start.6) | collective-permute-done | bytes 393248 | tf_op jit(solution)/shard_map/ppermute | solution.py:36
  56.6 6.3 %product.1 = (bf16[128,1536]{1,0:T(8,128)(2,1)S(1)}, bf16[128,1536]{1,0:T(8,128)(2,1)S(1)}, bf16[128,1536]{1,0:T(8,128)(2,1)S(1)}, bf16[128,1536]{1,0:T(8,128)(2,1)S(1)}) custom-call(s32[4]{0:T(128)S(1)} %pad_add_fusion.2.place_ref, bf16[128,1536]{1,0:T(8,128)(2,1)} %get-tuple-element.22.refs_0_, bf16[128,1536]{1,0:T(8,128)(2,1)} %collective-permute-done.4.refs_1_, ...), custom_call_target="tpu_custom_call" | custom-call | flops 2415919104 | bytes 8388608 | tf_op jit(solution)/shard_map/product/pallas_call | solution.py:220
  67.2 2.5 %collective-permute-start.14 = (bf16[128,1536]{1,0:T(8,128)(2,1)S(1)}, bf16[128,1536]{1,0:T(8,128)(2,1)}, u32[]{:S(2)}, u32[]{:S(2)}) collective-permute-start(bf16[128,1536]{1,0:T(8,128)(2,1)S(1)} %get-tuple-element.28), channel_id=1, source_target_pairs={{0,16},{32,48},{2,18},{34,50},{4,20},{36,52},{6,22},{38,54},{1,17}... | collective-permute-start | bytes 1179656 | tf_op jit(solution)/shard_map/ppermute | solution.py:36
  70.8 2.5 %put.6 = bf16[1536,1536]{1,0:T(8,128)(2,1)S(1)} custom-call(s32[4]{0:T(128)S(1)} %pad_add_fusion.1.index_ref, bf16[384,1536]{1,0:T(8,128)(2,1)S(1)} %get-tuple-element.43.refs_0_, bf16[384,1536]{1,0:T(8,128)(2,1)} %collective-permute-done.7.refs_1_, bf16[384,1536]{1,0:T(8,128)(2,1)} %collective-permute-done.8.refs_2_, ...), custom_call_target="tpu_custom_call" | custom-call | tf_op jit(solution)/shard_map/put/pallas_call | solution.py:171
  76.6 5.4 %convolution_convert_fusion.5 = bf16[512,1536]{1,0:T(8,128)(2,1)S(1)} fusion(bf16[512,1536]{1,0:T(8,128)(2,1)} %all-gather.2.cloned.1.call-done, bf16[1536,1536]{1,0:T(8,128)(2,1)} %copy-done.2), kind=kOutput, calls=%fused_computation.6 | convolution fusion | flops 2416705536 | bytes 7864320 | tf_op jit(solution)/shard_map/dot_general | solution.py:40
  84.5 2.4 %collective-permute-start.11 = (bf16[128,1536]{1,0:T(8,128)(2,1)S(1)}, bf16[128,1536]{1,0:T(8,128)(2,1)S(1)}, u32[]{:S(2)}, u32[]{:S(2)}) collective-permute-start(bf16[128,1536]{1,0:T(8,128)(2,1)S(1)} %get-tuple-element.53), channel_id=1, source_target_pairs={{0,16},{32,48},{2,18},{34,50},{4,20},{36,52},{6,22},{38,54},{1,17}... | collective-permute-start | bytes 1179656 | tf_op jit(solution)/shard_map/ppermute | solution.py:36
  88.1 8.2 %collective-permute-done.10 = bf16[128,1536]{1,0:T(8,128)(2,1)S(1)} collective-permute-done((bf16[128,1536]{1,0:T(8,128)(2,1)S(1)}, bf16[128,1536]{1,0:T(8,128)(2,1)S(1)}, u32[]{:S(2)}, u32[]{:S(2)}) %collective-permute-start.10) | collective-permute-done | bytes 393248 | tf_op jit(solution)/shard_map/ppermute | solution.py:36
  96.3 7.6 %collective-permute-done.11 = bf16[128,1536]{1,0:T(8,128)(2,1)S(1)} collective-permute-done((bf16[128,1536]{1,0:T(8,128)(2,1)S(1)}, bf16[128,1536]{1,0:T(8,128)(2,1)S(1)}, u32[]{:S(2)}, u32[]{:S(2)}) %collective-permute-start.11) | collective-permute-done | bytes 393248 | tf_op jit(solution)/shard_map/ppermute | solution.py:36
  106.1 3.2 %collective-permute-start.16 = (bf16[128,1536]{1,0:T(8,128)(2,1)S(1)}, bf16[128,1536]{1,0:T(8,128)(2,1)S(1)}, u32[]{:S(2)}, u32[]{:S(2)}) collective-permute-start(bf16[128,1536]{1,0:T(8,128)(2,1)S(1)} %get-tuple-element.39.refs_0_), channel_id=1, source_target_pairs={{0,24},{32,56},{2,26},{34,58},{4,28},{36,60},{6,30},{38,62},{1,25}... | collective-permute-start | bytes 1179656 | tf_op jit(solution)/shard_map/ppermute | solution.py:36
  110.1 2.5 %constant_dynamic-slice_fusion.3 = (bf16[512,384]{1,0:T(8,128)(2,1)}, bf16[512,384]{1,0:T(8,128)(2,1)S(1)}, bf16[512,384]{1,0:T(8,128)(2,1)S(1)}, bf16[512,384]{1,0:T(8,128)(2,1)}) fusion(bf16[512,1536]{1,0:T(8,128)(2,1)} %all-gather.2.cloned.1.call-done, s32[]{:T(128)S(6)} %select_n.127, s32[]{:T(128)S(6)} %select_n.130, s32[]{:T(128)S(6)} %select_n.129, ...), kind=kLoop, calls=%fused_computation.47 | loop fusion | bytes 3145744 | tf_op jit(solution)/shard_map/dynamic_slice | solution.py:295
  112.5 13.1 %collective-permute-done.16.refs_1_ = bf16[128,1536]{1,0:T(8,128)(2,1)S(1)} collective-permute-done((bf16[128,1536]{1,0:T(8,128)(2,1)S(1)}, bf16[128,1536]{1,0:T(8,128)(2,1)S(1)}, u32[]{:S(2)}, u32[]{:S(2)}) %collective-permute-start.16) | collective-permute-done | bytes 393248 | tf_op jit(solution)/shard_map/ppermute | solution.py:36
  125.6 4.4 %collective-permute-done.18.refs_3_ = bf16[128,1536]{1,0:T(8,128)(2,1)S(1)} collective-permute-done((bf16[128,1536]{1,0:T(8,128)(2,1)S(1)}, bf16[128,1536]{1,0:T(8,128)(2,1)S(1)}, u32[]{:S(2)}, u32[]{:S(2)}) %collective-permute-start.18) | collective-permute-done | bytes 393248 | tf_op jit(solution)/shard_map/ppermute | solution.py:36
  131.4 2.8 %convolution_convert_fusion.1 = bf16[768,1536]{1,0:T(8,128)(2,1)} fusion(bf16[512,1536]{1,0:T(8,128)(2,1)S(1)} %put.7, bf16[512,384]{1,0:T(8,128)(2,1)S(1)} %get-tuple-element.48, bf16[512,384]{1,0:T(8,128)(2,1)S(1)} %get-tuple-element.49), kind=kOutput, calls=%fused_computation.2 | convolution fusion | flops 1210712064 | bytes 4718592 | tf_op jit(solution)/shard_map/dot_general | solution.py:40
  134.8 3.8 %convolution_convert_fusion.4 = bf16[512,1536]{1,0:T(8,128)(2,1)} fusion(bf16[512,1536]{1,0:T(8,128)(2,1)S(1)} %put.7, bf16[1536,1536]{1,0:T(8,128)(2,1)S(1)} %bitcast.60), kind=kOutput, calls=%fused_computation.5 | convolution fusion | flops 2416705536 | bytes 7864320 | tf_op jit(solution)/shard_map/dot_general | solution.py:40
  144.4 2.5 %add_convert_fusion = bf16[768,1536]{1,0:T(8,128)(2,1)S(1)} fusion(bf16[768,1536]{1,0:T(8,128)(2,1)} %collective-permute-done.19, bf16[768,1536]{1,0:T(8,128)(2,1)S(1)} %convolution_convert_fusion.2), kind=kLoop, calls=%fused_computation.1 | loop fusion | flops 4718592 | bytes 7077888 | tf_op jit(solution)/shard_map/convert_element_type | solution.py:304
  148.2 3.8 %collective-permute-done.20.refs_1_ = bf16[128,1536]{1,0:T(8,128)(2,1)S(1)} collective-permute-done((bf16[128,1536]{1,0:T(8,128)(2,1)S(1)}, bf16[128,1536]{1,0:T(8,128)(2,1)S(1)}, u32[]{:S(2)}, u32[]{:S(2)}) %collective-permute-start.20) | collective-permute-done | bytes 393248 | tf_op jit(solution)/shard_map/ppermute | solution.py:36
  153.5 9.4 %collective-permute-done.22.refs_3_ = bf16[128,1536]{1,0:T(8,128)(2,1)S(1)} collective-permute-done((bf16[128,1536]{1,0:T(8,128)(2,1)S(1)}, bf16[128,1536]{1,0:T(8,128)(2,1)S(1)}, u32[]{:S(2)}, u32[]{:S(2)}) %collective-permute-start.22) | collective-permute-done | bytes 393248 | tf_op jit(solution)/shard_map/ppermute | solution.py:36
  164.3 4.4 %convolution_convert_fusion = bf16[1536,1536]{1,0:T(8,128)(2,1)} fusion(bf16[512,1536]{1,0:T(8,128)(2,1)S(1)} %put.8, bf16[512,1536]{1,0:T(8,128)(2,1)S(1)} %put.9), kind=kOutput, calls=%fused_computation | convolution fusion | flops 2418278400 | bytes 7864320 | tf_op jit(solution)/shard_map/dot_general | solution.py:40
  168.8 2.8 %collective-permute-start.26 = (bf16[384,1536]{1,0:T(8,128)(2,1)}, bf16[384,1536]{1,0:T(8,128)(2,1)}, u32[]{:S(2)}, u32[]{:S(2)}) collective-permute-start(bf16[384,1536]{1,0:T(8,128)(2,1)} %get-tuple-element.41), channel_id=1, source_target_pairs={{0,64},{32,96},{2,66},{34,98},{4,68},{36,100},{6,70},{38,102},{1,6... | collective-permute-start | bytes 3538952 | tf_op jit(solution)/shard_map/ppermute | solution.py:36
  171.6 4.9 %convolution_convert_fusion.3 = bf16[512,1536]{1,0:T(8,128)(2,1)S(1)} fusion(bf16[512,1536]{1,0:T(8,128)(2,1)S(1)} %put.8, bf16[1536,1536]{1,0:T(8,128)(2,1)} %copy-done.1), kind=kOutput, calls=%fused_computation.4 | convolution fusion | flops 2416705536 | bytes 7864320 | tf_op jit(solution)/shard_map/dot_general | solution.py:40
  180.9 8.5 %collective-permute-done.23 = bf16[128,1536]{1,0:T(8,128)(2,1)S(1)} collective-permute-done((bf16[128,1536]{1,0:T(8,128)(2,1)S(1)}, bf16[128,1536]{1,0:T(8,128)(2,1)S(1)}, u32[]{:S(2)}, u32[]{:S(2)}) %collective-permute-start.23) | collective-permute-done | bytes 393248 | tf_op jit(solution)/shard_map/ppermute | solution.py:36
  189.4 7.6 %collective-permute-done.24 = bf16[128,1536]{1,0:T(8,128)(2,1)S(1)} collective-permute-done((bf16[128,1536]{1,0:T(8,128)(2,1)S(1)}, bf16[128,1536]{1,0:T(8,128)(2,1)S(1)}, u32[]{:S(2)}, u32[]{:S(2)}) %collective-permute-start.24) | collective-permute-done | bytes 393248 | tf_op jit(solution)/shard_map/ppermute | solution.py:36
  199.2 3.3 %copied.1.refs_4_ = bf16[384,3072]{1,0:T(8,128)(2,1)} custom-call(s32[6]{0:T(128)S(1)} %pad_add_fusion.4.refs_0_, bf16[384,1536]{1,0:T(8,128)(2,1)S(1)} %get-tuple-element.40.refs_1_, bf16[384,1536]{1,0:T(8,128)(2,1)} %collective-permute-done.26.refs_2_), custom_call_target="tpu_custom_call" | custom-call | flops 1024 | bytes 1024 | tf_op jit(solution)/shard_map/copied/pallas_call | solution.py:66
  206.3 2.5 %collective-permute-done.29.refs_3_ = bf16[64,1536]{1,0:T(8,128)(2,1)S(1)} collective-permute-done((bf16[64,1536]{1,0:T(8,128)(2,1)S(1)}, bf16[64,1536]{1,0:T(8,128)(2,1)S(1)}, u32[]{:S(2)}, u32[]{:S(2)}) %collective-permute-start.29) | collective-permute-done | bytes 196640 | tf_op jit(solution)/shard_map/ppermute | solution.py:36
  208.8 2.3 %collective-permute-done.28.refs_2_ = bf16[64,1536]{1,0:T(8,128)(2,1)S(1)} collective-permute-done((bf16[64,1536]{1,0:T(8,128)(2,1)S(1)}, bf16[64,1536]{1,0:T(8,128)(2,1)S(1)}, u32[]{:S(2)}, u32[]{:S(2)}) %collective-permute-start.28) | collective-permute-done | bytes 196640 | tf_op jit(solution)/shard_map/ppermute | solution.py:36
  211.1 5.6 %collective-permute-done.27.refs_1_ = bf16[64,1536]{1,0:T(8,128)(2,1)S(1)} collective-permute-done((bf16[64,1536]{1,0:T(8,128)(2,1)S(1)}, bf16[64,1536]{1,0:T(8,128)(2,1)S(1)}, u32[]{:S(2)}, u32[]{:S(2)}) %collective-permute-start.27) | collective-permute-done | bytes 196640 | tf_op jit(solution)/shard_map/ppermute | solution.py:36
  (100 shorter events, 49.9 us)
Async XLA Ops:
  7.2 69.5 %all-gather.2.cloned.1.call-start = ((), (), s32[]{:S(2)}) async-start(), calls=%async_computation.2 | async-start | bytes 1966080 | tf_op jit(solution)/shard_map/all_gather | solution.py:276
  7.2 18.7 %collective-permute-start.3 = (bf16[768,1536]{1,0:T(8,128)(2,1)}, bf16[768,1536]{1,0:T(8,128)(2,1)S(1)}, u32[]{:S(2)}, u32[]{:S(2)}) collective-permute-start(bf16[768,1536]{1,0:T(8,128)(2,1)} %refs_0_.1), channel_id=1, source_target_pairs={{0,32},{32,0},{2,34},{34,2},{4,36},{36,4},{6,38},{38,6},{1,33},{33... | collective-permute-start | bytes 7077896 | tf_op jit(solution)/shard_map/ppermute | solution.py:36
  10.5 11.2 %collective-permute-start = (bf16[64,1536]{1,0:T(8,128)(2,1)S(1)}, bf16[64,1536]{1,0:T(8,128)(2,1)S(1)}, u32[]{:S(2)}, u32[]{:S(2)}) collective-permute-start(bf16[64,1536]{1,0:T(8,128)(2,1)S(1)} %constant_dynamic-update-slice_fusion.refs_0_), channel_id=1, source_target_pairs={{0,65},{32,97},{2,67},{34,99},{4,69},{36,101},{6,71},{38,103},{1,0... | collective-permute-start | bytes 589832 | tf_op jit(solution)/shard_map/ppermute | solution.py:36
  13.3 8.4 %collective-permute-start.1 = (bf16[64,1536]{1,0:T(8,128)(2,1)S(1)}, bf16[64,1536]{1,0:T(8,128)(2,1)S(1)}, u32[]{:S(2)}, u32[]{:S(2)}) collective-permute-start(bf16[64,1536]{1,0:T(8,128)(2,1)S(1)} %constant_dynamic-update-slice_fusion.refs_0_), channel_id=1, source_target_pairs={{0,64},{32,96},{2,66},{34,98},{4,68},{36,100},{6,70},{38,102},{1,6... | collective-permute-start | bytes 589832 | tf_op jit(solution)/shard_map/ppermute | solution.py:36
  13.7 12.2 %collective-permute-start.2 = (bf16[64,1536]{1,0:T(8,128)(2,1)S(1)}, bf16[64,1536]{1,0:T(8,128)(2,1)S(1)}, u32[]{:S(2)}, u32[]{:S(2)}) collective-permute-start(bf16[64,1536]{1,0:T(8,128)(2,1)S(1)} %constant_dynamic-update-slice_fusion.refs_0_), channel_id=1, source_target_pairs={{0,1},{32,33},{2,3},{34,35},{4,5},{36,37},{6,7},{38,39},{1,64},{33... | collective-permute-start | bytes 589832 | tf_op jit(solution)/shard_map/ppermute | solution.py:36
  28.4 20.3 %collective-permute-start.4 = (bf16[128,1536]{1,0:T(8,128)(2,1)}, bf16[128,1536]{1,0:T(8,128)(2,1)}, u32[]{:S(2)}, u32[]{:S(2)}) collective-permute-start(bf16[128,1536]{1,0:T(8,128)(2,1)} %get-tuple-element.22.refs_0_), channel_id=1, source_target_pairs={{0,6},{32,38},{2,0},{34,32},{4,2},{36,34},{6,4},{38,36},{1,7},{33,... | collective-permute-start | bytes 1179656 | tf_op jit(solution)/shard_map/ppermute | solution.py:36
  32.2 16.6 %collective-permute-start.5 = (bf16[128,1536]{1,0:T(8,128)(2,1)}, bf16[128,1536]{1,0:T(8,128)(2,1)}, u32[]{:S(2)}, u32[]{:S(2)}) collective-permute-start(bf16[128,1536]{1,0:T(8,128)(2,1)} %get-tuple-element.22.refs_0_), channel_id=1, source_target_pairs={{0,4},{32,36},{2,6},{34,38},{4,0},{36,32},{6,2},{38,34},{1,5},{33,... | collective-permute-start | bytes 1179656 | tf_op jit(solution)/shard_map/ppermute | solution.py:36
  32.2 20.7 %collective-permute-start.6 = (bf16[128,1536]{1,0:T(8,128)(2,1)}, bf16[128,1536]{1,0:T(8,128)(2,1)}, u32[]{:S(2)}, u32[]{:S(2)}) collective-permute-start(bf16[128,1536]{1,0:T(8,128)(2,1)} %get-tuple-element.22.refs_0_), channel_id=1, source_target_pairs={{0,2},{32,34},{2,4},{34,36},{4,6},{36,38},{6,0},{38,32},{1,3},{33,... | collective-permute-start | bytes 1179656 | tf_op jit(solution)/shard_map/ppermute | solution.py:36
  35.7 27.9 %collective-permute-start.7 = (bf16[384,1536]{1,0:T(8,128)(2,1)}, bf16[384,1536]{1,0:T(8,128)(2,1)}, u32[]{:S(2)}, u32[]{:S(2)}) collective-permute-start(bf16[384,1536]{1,0:T(8,128)(2,1)} %get-tuple-element.24), channel_id=1, source_target_pairs={{0,64},{32,96},{2,66},{34,98},{4,68},{36,100},{6,70},{38,102},{1,6... | collective-permute-start | bytes 3538952 | tf_op jit(solution)/shard_map/ppermute | solution.py:36
  52.9 149.8 %reduce-scatter.3.cloned.1.call-start = ((), (), s32[]{:S(2)}) async-start(), calls=%async_computation.3 | async-start | bytes 1966080 | tf_op jit(solution)/shard_map/reduce_scatter | solution.py:303
  52.9 17.9 %collective-permute-start.8 = (bf16[384,1536]{1,0:T(8,128)(2,1)S(1)}, bf16[384,1536]{1,0:T(8,128)(2,1)}, u32[]{:S(2)}, u32[]{:S(2)}) collective-permute-start(bf16[384,1536]{1,0:T(8,128)(2,1)S(1)} %get-tuple-element.43.refs_0_), channel_id=1, source_target_pairs={{0,32},{32,0},{2,34},{34,2},{4,36},{36,4},{6,38},{38,6},{1,33},{33... | collective-permute-start | bytes 3538952 | tf_op jit(solution)/shard_map/ppermute | solution.py:36
  63.6 7.2 %collective-permute-start.9 = (bf16[384,1536]{1,0:T(8,128)(2,1)}, bf16[384,1536]{1,0:T(8,128)(2,1)S(1)}, u32[]{:S(2)}, u32[]{:S(2)}) collective-permute-start(bf16[384,1536]{1,0:T(8,128)(2,1)} %collective-permute-done.7.refs_1_), channel_id=1, source_target_pairs={{0,32},{32,0},{2,34},{34,2},{4,36},{36,4},{6,38},{38,6},{1,33},{33... | collective-permute-start | bytes 3538952 | tf_op jit(solution)/shard_map/ppermute | solution.py:36
  66.0 21.0 %collective-permute-start.13 = (bf16[128,1536]{1,0:T(8,128)(2,1)}, bf16[128,1536]{1,0:T(8,128)(2,1)}, u32[]{:S(2)}, u32[]{:S(2)}) collective-permute-start(bf16[128,1536]{1,0:T(8,128)(2,1)} %copy-done.5), channel_id=1, source_target_pairs={{0,8},{32,40},{2,10},{34,42},{4,12},{36,44},{6,14},{38,46},{1,9},{... | collective-permute-start | bytes 1179656 | tf_op jit(solution)/shard_map/ppermute | solution.py:36
  67.2 20.9 %collective-permute-start.14 = (bf16[128,1536]{1,0:T(8,128)(2,1)S(1)}, bf16[128,1536]{1,0:T(8,128)(2,1)}, u32[]{:S(2)}, u32[]{:S(2)}) collective-permute-start(bf16[128,1536]{1,0:T(8,128)(2,1)S(1)} %get-tuple-element.28), channel_id=1, source_target_pairs={{0,16},{32,48},{2,18},{34,50},{4,20},{36,52},{6,22},{38,54},{1,17}... | collective-permute-start | bytes 1179656 | tf_op jit(solution)/shard_map/ppermute | solution.py:36
  69.6 18.5 %collective-permute-start.15 = (bf16[128,1536]{1,0:T(8,128)(2,1)S(1)}, bf16[128,1536]{1,0:T(8,128)(2,1)}, u32[]{:S(2)}, u32[]{:S(2)}) collective-permute-start(bf16[128,1536]{1,0:T(8,128)(2,1)S(1)} %get-tuple-element.29), channel_id=1, source_target_pairs={{0,24},{32,56},{2,26},{34,58},{4,28},{36,60},{6,30},{38,62},{1,25}... | collective-permute-start | bytes 1179656 | tf_op jit(solution)/shard_map/ppermute | solution.py:36
  83.3 13.0 %collective-permute-start.10 = (bf16[128,1536]{1,0:T(8,128)(2,1)S(1)}, bf16[128,1536]{1,0:T(8,128)(2,1)S(1)}, u32[]{:S(2)}, u32[]{:S(2)}) collective-permute-start(bf16[128,1536]{1,0:T(8,128)(2,1)S(1)} %get-tuple-element.51), channel_id=1, source_target_pairs={{0,8},{32,40},{2,10},{34,42},{4,12},{36,44},{6,14},{38,46},{1,9},{... | collective-permute-start | bytes 1179656 | tf_op jit(solution)/shard_map/ppermute | solution.py:36
  84.5 19.3 %collective-permute-start.11 = (bf16[128,1536]{1,0:T(8,128)(2,1)S(1)}, bf16[128,1536]{1,0:T(8,128)(2,1)S(1)}, u32[]{:S(2)}, u32[]{:S(2)}) collective-permute-start(bf16[128,1536]{1,0:T(8,128)(2,1)S(1)} %get-tuple-element.53), channel_id=1, source_target_pairs={{0,16},{32,48},{2,18},{34,50},{4,20},{36,52},{6,22},{38,54},{1,17}... | collective-permute-start | bytes 1179656 | tf_op jit(solution)/shard_map/ppermute | solution.py:36
  86.9 16.9 %collective-permute-start.12 = (bf16[128,1536]{1,0:T(8,128)(2,1)S(1)}, bf16[128,1536]{1,0:T(8,128)(2,1)S(1)}, u32[]{:S(2)}, u32[]{:S(2)}) collective-permute-start(bf16[128,1536]{1,0:T(8,128)(2,1)S(1)} %get-tuple-element.52), channel_id=1, source_target_pairs={{0,24},{32,56},{2,26},{34,58},{4,28},{36,60},{6,30},{38,62},{1,25}... | collective-permute-start | bytes 1179656 | tf_op jit(solution)/shard_map/ppermute | solution.py:36
  106.1 19.4 %collective-permute-start.16 = (bf16[128,1536]{1,0:T(8,128)(2,1)S(1)}, bf16[128,1536]{1,0:T(8,128)(2,1)S(1)}, u32[]{:S(2)}, u32[]{:S(2)}) collective-permute-start(bf16[128,1536]{1,0:T(8,128)(2,1)S(1)} %get-tuple-element.39.refs_0_), channel_id=1, source_target_pairs={{0,24},{32,56},{2,26},{34,58},{4,28},{36,60},{6,30},{38,62},{1,25}... | collective-permute-start | bytes 1179656 | tf_op jit(solution)/shard_map/ppermute | solution.py:36
  109.3 16.3 %collective-permute-start.17 = (bf16[128,1536]{1,0:T(8,128)(2,1)S(1)}, bf16[128,1536]{1,0:T(8,128)(2,1)S(1)}, u32[]{:S(2)}, u32[]{:S(2)}) collective-permute-start(bf16[128,1536]{1,0:T(8,128)(2,1)S(1)} %get-tuple-element.39.refs_0_), channel_id=1, source_target_pairs={{0,16},{32,48},{2,18},{34,50},{4,20},{36,52},{6,22},{38,54},{1,17}... | collective-permute-start | bytes 1179656 | tf_op jit(solution)/shard_map/ppermute | solution.py:36
  109.5 20.6 %collective-permute-start.18 = (bf16[128,1536]{1,0:T(8,128)(2,1)S(1)}, bf16[128,1536]{1,0:T(8,128)(2,1)S(1)}, u32[]{:S(2)}, u32[]{:S(2)}) collective-permute-start(bf16[128,1536]{1,0:T(8,128)(2,1)S(1)} %get-tuple-element.39.refs_0_), channel_id=1, source_target_pairs={{0,8},{32,40},{2,10},{34,42},{4,12},{36,44},{6,14},{38,46},{1,9},{... | collective-permute-start | bytes 1179656 | tf_op jit(solution)/shard_map/ppermute | solution.py:36
  134.2 5.1 %collective-permute-start.19 = (bf16[768,1536]{1,0:T(8,128)(2,1)}, bf16[768,1536]{1,0:T(8,128)(2,1)}, u32[]{:S(2)}, u32[]{:S(2)}) collective-permute-start(bf16[768,1536]{1,0:T(8,128)(2,1)} %convolution_convert_fusion.1), channel_id=1, source_target_pairs={{0,32},{32,0},{2,34},{34,2},{4,36},{36,4},{6,38},{38,6},{1,33},{33... | collective-permute-start | bytes 7077896 | tf_op jit(solution)/shard_map/ppermute | solution.py:36
  139.4 78.1 %reduce-scatter.5.cloned.1.call-start = ((), (), s32[]{:S(2)}) async-start(), calls=%async_computation.4 | async-start | bytes 7077888 | tf_op jit(solution)/shard_map/reduce_scatter | solution.py:311
  141.5 10.5 %collective-permute-start.20 = (bf16[128,1536]{1,0:T(8,128)(2,1)S(1)}, bf16[128,1536]{1,0:T(8,128)(2,1)S(1)}, u32[]{:S(2)}, u32[]{:S(2)}) collective-permute-start(bf16[128,1536]{1,0:T(8,128)(2,1)S(1)} %get-tuple-element.32.refs_0_), channel_id=1, source_target_pairs={{0,24},{32,56},{2,26},{34,58},{4,28},{36,60},{6,30},{38,62},{1,25}... | collective-permute-start | bytes 1179656 | tf_op jit(solution)/shard_map/ppermute | solution.py:36
  142.0 11.6 %collective-permute-start.21 = (bf16[128,1536]{1,0:T(8,128)(2,1)S(1)}, bf16[128,1536]{1,0:T(8,128)(2,1)S(1)}, u32[]{:S(2)}, u32[]{:S(2)}) collective-permute-start(bf16[128,1536]{1,0:T(8,128)(2,1)S(1)} %get-tuple-element.32.refs_0_), channel_id=1, source_target_pairs={{0,16},{32,48},{2,18},{34,50},{4,20},{36,52},{6,22},{38,54},{1,17}... | collective-permute-start | bytes 1179656 | tf_op jit(solution)/shard_map/ppermute | solution.py:36
  142.2 20.8 %collective-permute-start.22 = (bf16[128,1536]{1,0:T(8,128)(2,1)S(1)}, bf16[128,1536]{1,0:T(8,128)(2,1)S(1)}, u32[]{:S(2)}, u32[]{:S(2)}) collective-permute-start(bf16[128,1536]{1,0:T(8,128)(2,1)S(1)} %get-tuple-element.32.refs_0_), channel_id=1, source_target_pairs={{0,8},{32,40},{2,10},{34,42},{4,12},{36,44},{6,14},{38,46},{1,9},{... | collective-permute-start | bytes 1179656 | tf_op jit(solution)/shard_map/ppermute | solution.py:36
  168.8 30.5 %collective-permute-start.26 = (bf16[384,1536]{1,0:T(8,128)(2,1)}, bf16[384,1536]{1,0:T(8,128)(2,1)}, u32[]{:S(2)}, u32[]{:S(2)}) collective-permute-start(bf16[384,1536]{1,0:T(8,128)(2,1)} %get-tuple-element.41), channel_id=1, source_target_pairs={{0,64},{32,96},{2,66},{34,98},{4,68},{36,100},{6,70},{38,102},{1,6... | collective-permute-start | bytes 3538952 | tf_op jit(solution)/shard_map/ppermute | solution.py:36
  177.7 11.7 %collective-permute-start.23 = (bf16[128,1536]{1,0:T(8,128)(2,1)S(1)}, bf16[128,1536]{1,0:T(8,128)(2,1)S(1)}, u32[]{:S(2)}, u32[]{:S(2)}) collective-permute-start(bf16[128,1536]{1,0:T(8,128)(2,1)S(1)} %get-tuple-element.44), channel_id=1, source_target_pairs={{0,2},{32,34},{2,4},{34,36},{4,6},{36,38},{6,0},{38,32},{1,3},{33,... | collective-permute-start | bytes 1179656 | tf_op jit(solution)/shard_map/ppermute | solution.py:36
  177.9 19.1 %collective-permute-start.24 = (bf16[128,1536]{1,0:T(8,128)(2,1)S(1)}, bf16[128,1536]{1,0:T(8,128)(2,1)S(1)}, u32[]{:S(2)}, u32[]{:S(2)}) collective-permute-start(bf16[128,1536]{1,0:T(8,128)(2,1)S(1)} %get-tuple-element.46), channel_id=1, source_target_pairs={{0,4},{32,36},{2,6},{34,38},{4,0},{36,32},{6,2},{38,34},{1,5},{33,... | collective-permute-start | bytes 1179656 | tf_op jit(solution)/shard_map/ppermute | solution.py:36
  180.1 18.0 %collective-permute-start.25 = (bf16[128,1536]{1,0:T(8,128)(2,1)S(1)}, bf16[128,1536]{1,0:T(8,128)(2,1)S(1)}, u32[]{:S(2)}, u32[]{:S(2)}) collective-permute-start(bf16[128,1536]{1,0:T(8,128)(2,1)S(1)} %get-tuple-element.45), channel_id=1, source_target_pairs={{0,6},{32,38},{2,0},{34,32},{4,2},{36,34},{6,4},{38,36},{1,7},{33,... | collective-permute-start | bytes 1179656 | tf_op jit(solution)/shard_map/ppermute | solution.py:36
  204.9 6.2 %collective-permute-start.28 = (bf16[64,1536]{1,0:T(8,128)(2,1)S(1)}, bf16[64,1536]{1,0:T(8,128)(2,1)S(1)}, u32[]{:S(2)}, u32[]{:S(2)}) collective-permute-start(bf16[64,1536]{1,0:T(8,128)(2,1)S(1)} %pad_maximum_fusion.2), channel_id=1, source_target_pairs={{0,64},{32,96},{2,66},{34,98},{4,68},{36,100},{6,70},{38,102},{1,6... | collective-permute-start | bytes 589832 | tf_op jit(solution)/shard_map/ppermute | solution.py:36
  206.2 10.5 %collective-permute-start.27 = (bf16[64,1536]{1,0:T(8,128)(2,1)S(1)}, bf16[64,1536]{1,0:T(8,128)(2,1)S(1)}, u32[]{:S(2)}, u32[]{:S(2)}) collective-permute-start(bf16[64,1536]{1,0:T(8,128)(2,1)S(1)} %pad_maximum_fusion.1), channel_id=1, source_target_pairs={{0,1},{32,33},{2,3},{34,35},{4,5},{36,37},{6,7},{38,39},{1,64},{33... | collective-permute-start | bytes 589832 | tf_op jit(solution)/shard_map/ppermute | solution.py:36
  (13 other events, 48.2 us)
Sparse Core Ops, SparseCore 0:
  53.0 23.5 all-gather.1
  139.5 22.0 reduce-scatter.2
  168.9 12.6 reduce-scatter.4
where the time goes:
time: 225 us; the launch traced here: 224 us
  waiting for transfers between devices  106 us (47%)
  starting transfers between devices  37.3 us (17%)
  matrix products  22.8 us (10%)
  Pallas kernels  20.1 us (9%)
  local copies, waits for them, and re-layouts  17.2 us (8%)
  between operations  14.1 us (6%)
  other arithmetic  6.49 us (3%)
    ppermute x30, waiting for transfers between devices, shift(): return lax.ppermute(value, AXES, pairs)  105 us
    ppermute x30, starting transfers between devices, shift(): return lax.ppermute(value, AXES, pairs)  37.2 us
    dot_general x6, matrix products, mul(): lax.dot_general(left, right, dims, preferred_element_type=F32).astype(BF16)  22.8 us
    unnamed x25, local copies, waits for them, and re-layouts  8.52 us
    pallas_call x5, Pallas kernels, put(): pl.pallas_call(kernel, out_shape=[jax.ShapeDtypeStruct((n * rows, width),...  7.97 us
    pallas_call x1, Pallas kernels, product(): pl.pallas_call(kernel, grid=(1536 // wide,), out_shape=out_shape, in_spec...  6.27 us
    pallas_call x3, Pallas kernels, call(): pl.pallas_call(waiting, grid=grid, out_shape=[jax.ShapeDtypeStruct(shape,...  5.9 us
  transfers between devices with their start and end apart: 33, of which 19 were waited for; matrix products, arithmetic and copies ran while one was open for 15% of the time, Pallas kernels for 8%

commit v1 on v0

--- a/solution.py
+++ b/solution.py
@@ -240,9 +240,13 @@
     return result
 
 
+def terms_of(rows, me, axis):
+    blocks = rows.reshape(4, rows.shape[0] // 4, rows.shape[1])
+    return [at(blocks, me)] + [shift(at(blocks, (me + i) % 4), **{axis: i}) for i in (1, 2, 3)]
+
+
 def summed(rows, me, axis):
-    blocks = rows.reshape(4, rows.shape[0] // 4, rows.shape[1])
-    return total([at(blocks, me)] + [shift(at(blocks, (me + i) % 4), **{axis: i}) for i in (1, 2, 3)])
+    return total(terms_of(rows, me, axis))
 
 
 def scatter(parts, axis):
@@ -270,7 +274,7 @@
     away = shift(after(lax.dynamic_slice(in_weight, (0, (1 - b) * units), (384, units)), grad_128), dy=2)
 
     (out_tile,) = put([(c, out_weight), (1 - c, out_other)])
-    grad_parts = product(grad_blocks, to_x, out_tile, BACK_DIMS)
+    *grad_parts, grad_rows = product(grad_blocks, to_x, out_tile, BACK_DIMS, True)
     grad_act = total(scatter(grad_parts, "dx"))
 
     tok_rows = lax.all_gather(after(tok_128, *grad_blocks), "z", axis=0, tiled=True)
@@ -299,17 +303,16 @@
 
     other = shift(mul(tok_other, grad_pre, LEAD_DIMS), fc=1)
     in_part = mul(grad_pre, in_tile, BACK_DIMS)
-    other, in_part = lax.optimization_barrier((other, in_part))
     in_rows = lax.psum_scatter(in_part, "z", scatter_dimension=0, tiled=True)
     rows = total([mul(tok_mine, grad_pre, LEAD_DIMS), other]).astype(BF16).reshape(2, 384, units)
     kept, sent = at(rows, b), at(rows, 1 - b)
     arrived = shift(sent, dy=2)
     act_blocks[0] = after(act_blocks[0], sent)
-    (act_rows,) = put(list(zip(in_z, act_blocks)))
-    (grad_rows,) = put([((z + i) % 4, grad_blocks[i]) for i in range(4)])
-    out_rows = summed(mul(act_rows, out_tile, PLAIN_DIMS), z, "dz").astype(BF16)
+    (act_rows,) = put(list(enumerate(act_blocks)))
+    out_terms = terms_of(mul(act_rows, out_tile, PLAIN_DIMS), (z - x) % 4, "dz")
     grad_w_out = lax.psum_scatter(mul(act_rows, grad_rows, LEAD_DIMS), "c", scatter_dimension=0, tiled=True)
-    out_rows, arrived = lax.optimization_barrier((out_rows, arrived))
+    out_terms[1], arrived = lax.optimization_barrier((out_terms[1], arrived))
+    out_rows = total(out_terms).astype(BF16)
     grad_w_in = copied((384, 2 * units), [(kept, 0, 0, b), (arrived, 0, 0, 1 - b)])
     parts = [jnp.concatenate([v[i * 32 : (i + 1) * 32] for v in (out_rows, in_rows)]) for i in range(4)]
     return (*last(scatter(parts, "dy"), [grad_w_in]), grad_w_in, grad_w_out)

time: 225 us -> 221 us (0.982)
  starting transfers between devices: 37.3 us -> 30.6 us
  local copies, waits for them, and re-layouts: 17.2 us -> 20 us
    ppermute x30, starting transfers between devices: 37.2 us -> 30.5 us  [shift(): return lax.ppermute(value, AXES, pairs)]
    unnamed x25 -> x29, local copies, waits for them, and re-layouts: 8.52 us -> 11.5 us
    pallas_call x5 -> x4, Pallas kernels: 7.97 us -> 6.04 us  [put(): pl.pallas_call(kernel, out_shape=[jax.ShapeDtypeStruct((n * rows, width),...]
  transfers between devices with their start and end apart: 33 -> 33, of which waited for: 19 -> 19; matrix products, arithmetic and copies ran while one was open for 15% -> 15% of each run, Pallas kernels for 8% -> 7%
where the time goes in v1:
time: 221 us; the launch traced here: 220 us
  waiting for transfers between devices  108 us (49%)
  starting transfers between devices  30.6 us (14%)
  matrix products  22.7 us (10%)
  local copies, waits for them, and re-layouts  20 us (9%)
  Pallas kernels  18.2 us (8%)
  between operations  14.1 us (6%)
  other arithmetic  6.17 us (3%)
    ppermute x30, waiting for transfers between devices, shift(): return lax.ppermute(value, AXES, pairs)  106 us
    ppermute x30, starting transfers between devices, shift(): return lax.ppermute(value, AXES, pairs)  30.5 us
    dot_general x6, matrix products, mul(): lax.dot_general(left, right, dims, preferred_element_type=F32).astype(BF16)  22.7 us
    unnamed x29, local copies, waits for them, and re-layouts  11.5 us
    pallas_call x1, Pallas kernels, product(): pl.pallas_call(kernel, grid=(1536 // wide,), out_shape=out_shape, in_spec...  6.29 us
    pallas_call x4, Pallas kernels, put(): pl.pallas_call(kernel, out_shape=[jax.ShapeDtypeStruct((n * rows, width),...  6.04 us
    pallas_call x3, Pallas kernels, call(): pl.pallas_call(waiting, grid=grid, out_shape=[jax.ShapeDtypeStruct(shape,...  5.89 us
  transfers between devices with their start and end apart: 33, of which 19 were waited for; matrix products, arithmetic and copies ran while one was open for 15% of the time, Pallas kernels for 7%

profile of v1, /device:TPU:1, one launch (start us, length us, event | category | flops | bytes accessed | tf_op | source)
XLA Modules:
  0.0 219.7 jit_solution(3626166349898497320)
XLA Ops:
  10.5 2.8 %collective-permute-start = (bf16[64,1536]{1,0:T(8,128)(2,1)S(1)}, bf16[64,1536]{1,0:T(8,128)(2,1)S(1)}, u32[]{:S(2)}, u32[]{:S(2)}) collective-permute-start(bf16[64,1536]{1,0:T(8,128)(2,1)S(1)} %constant_dynamic-update-slice_fusion.refs_0_), channel_id=1, source_target_pairs={{0,65},{32,97},{2,67},{34,99},{4,69},{36,101},{6,71},{38,103},{1,0... | collective-permute-start | bytes 589832 | tf_op jit(solution)/shard_map/ppermute | solution.py:36
  14.4 7.3 %collective-permute-done.refs_1_ = bf16[64,1536]{1,0:T(8,128)(2,1)S(1)} collective-permute-done((bf16[64,1536]{1,0:T(8,128)(2,1)S(1)}, bf16[64,1536]{1,0:T(8,128)(2,1)S(1)}, u32[]{:S(2)}, u32[]{:S(2)}) %collective-permute-start) | collective-permute-done | bytes 196640 | tf_op jit(solution)/shard_map/ppermute | solution.py:36
  21.7 4.1 %collective-permute-done.2.refs_3_ = bf16[64,1536]{1,0:T(8,128)(2,1)S(1)} collective-permute-done((bf16[64,1536]{1,0:T(8,128)(2,1)S(1)}, bf16[64,1536]{1,0:T(8,128)(2,1)S(1)}, u32[]{:S(2)}, u32[]{:S(2)}) %collective-permute-start.2) | collective-permute-done | bytes 196640 | tf_op jit(solution)/shard_map/ppermute | solution.py:36
  28.4 3.8 %collective-permute-start.4 = (bf16[128,1536]{1,0:T(8,128)(2,1)}, bf16[128,1536]{1,0:T(8,128)(2,1)}, u32[]{:S(2)}, u32[]{:S(2)}) collective-permute-start(bf16[128,1536]{1,0:T(8,128)(2,1)} %get-tuple-element.21.refs_0_), channel_id=1, source_target_pairs={{0,6},{32,38},{2,0},{34,32},{4,2},{36,34},{6,4},{38,36},{1,7},{33,... | collective-permute-start | bytes 1179656 | tf_op jit(solution)/shard_map/ppermute | solution.py:36
  32.9 2.8 %constant_dynamic-slice_fusion.4 = (bf16[384,1536]{1,0:T(8,128)(2,1)}, bf16[384,1536]{1,0:T(8,128)(2,1)S(1)}) fusion(bf16[384,3072]{1,0:T(8,128)(2,1)} %param.5, s32[]{:T(128)S(6)} %select_n.106, s32[]{:T(128)S(6)} %select_n.105), kind=kLoop, calls=%fused_computation.48 | loop fusion | bytes 4718600 | tf_op jit(solution)/shard_map/dynamic_slice | solution.py:274
  36.0 12.7 %collective-permute-done.4.refs_1_ = bf16[128,1536]{1,0:T(8,128)(2,1)} collective-permute-done((bf16[128,1536]{1,0:T(8,128)(2,1)}, bf16[128,1536]{1,0:T(8,128)(2,1)}, u32[]{:S(2)}, u32[]{:S(2)}) %collective-permute-start.4) | collective-permute-done | bytes 393248 | tf_op jit(solution)/shard_map/ppermute | solution.py:36
  48.8 4.1 %collective-permute-done.6.refs_3_ = bf16[128,1536]{1,0:T(8,128)(2,1)} collective-permute-done((bf16[128,1536]{1,0:T(8,128)(2,1)}, bf16[128,1536]{1,0:T(8,128)(2,1)}, u32[]{:S(2)}, u32[]{:S(2)}) %collective-permute-start.6) | collective-permute-done | bytes 393248 | tf_op jit(solution)/shard_map/ppermute | solution.py:36
  56.6 6.3 %product.1 = (bf16[128,1536]{1,0:T(8,128)(2,1)S(1)}, bf16[128,1536]{1,0:T(8,128)(2,1)S(1)}, bf16[128,1536]{1,0:T(8,128)(2,1)S(1)}, bf16[128,1536]{1,0:T(8,128)(2,1)S(1)}, bf16[512,1536]{1,0:T(8,128)(2,1)S(1)}) custom-call(s32[4]{0:T(128)S(1)} %pad_add_fusion.1.place_ref, bf16[128,1536]{1,0:T(8,128)(2,1)} %get-tuple-element.21.refs_0_, ...), custom_call_target="tpu_custom_call" | custom-call | flops 2415919104 | bytes 8388608 | tf_op jit(solution)/shard_map/product/pallas_call | solution.py:220
  66.0 2.5 %collective-permute-start.15 = (bf16[128,1536]{1,0:T(8,128)(2,1)}, bf16[128,1536]{1,0:T(8,128)(2,1)}, u32[]{:S(2)}, u32[]{:S(2)}) collective-permute-start(bf16[128,1536]{1,0:T(8,128)(2,1)} %copy-done.5), channel_id=1, source_target_pairs={{0,24},{32,56},{2,26},{34,58},{4,28},{36,60},{6,30},{38,62},{1,25}... | collective-permute-start | bytes 1179656 | tf_op jit(solution)/shard_map/ppermute | solution.py:36
  69.6 2.5 %put.5 = bf16[1536,1536]{1,0:T(8,128)(2,1)S(1)} custom-call(s32[4]{0:T(128)S(1)} %pad_add_fusion.index_ref, bf16[384,1536]{1,0:T(8,128)(2,1)S(1)} %get-tuple-element.41.refs_0_, bf16[384,1536]{1,0:T(8,128)(2,1)} %collective-permute-done.7.refs_1_, bf16[384,1536]{1,0:T(8,128)(2,1)} %collective-permute-done.8.refs_2_, ...), custom_call_target="tpu_custom_call" | custom-call | tf_op jit(solution)/shard_map/put/pallas_call | solution.py:171
  74.3 2.3 %all-gather.2.cloned.1.call-done = bf16[512,1536]{1,0:T(8,128)(2,1)} async-done(((bf16[128,1536]{1,0:T(8,128)(2,1)}), bf16[512,1536]{1,0:T(8,128)(2,1)}) %all-gather.2.cloned.1.call-update) | async-done | bytes 1572880 | tf_op jit(solution)/shard_map/all_gather | solution.py:280
  76.6 5.4 %convolution_convert_fusion.5 = bf16[512,1536]{1,0:T(8,128)(2,1)S(1)} fusion(bf16[512,1536]{1,0:T(8,128)(2,1)} %all-gather.2.cloned.1.call-done, bf16[1536,1536]{1,0:T(8,128)(2,1)} %copy-done.2), kind=kOutput, calls=%fused_computation.6 | convolution fusion | flops 2416705536 | bytes 7864320 | tf_op jit(solution)/shard_map/dot_general | solution.py:40
  83.3 2.5 %collective-permute-start.12 = (bf16[128,1536]{1,0:T(8,128)(2,1)S(1)}, bf16[128,1536]{1,0:T(8,128)(2,1)S(1)}, u32[]{:S(2)}, u32[]{:S(2)}) collective-permute-start(bf16[128,1536]{1,0:T(8,128)(2,1)S(1)} %get-tuple-element.50), channel_id=1, source_target_pairs={{0,24},{32,56},{2,26},{34,58},{4,28},{36,60},{6,30},{38,62},{1,25}... | collective-permute-start | bytes 1179656 | tf_op jit(solution)/shard_map/ppermute | solution.py:36
  86.9 2.6 %collective-permute-done.13 = bf16[128,1536]{1,0:T(8,128)(2,1)} collective-permute-done((bf16[128,1536]{1,0:T(8,128)(2,1)S(1)}, bf16[128,1536]{1,0:T(8,128)(2,1)}, u32[]{:S(2)}, u32[]{:S(2)}) %collective-permute-start.13) | collective-permute-done | bytes 393248 | tf_op jit(solution)/shard_map/ppermute | solution.py:36
  89.5 4.7 %collective-permute-done.12 = bf16[128,1536]{1,0:T(8,128)(2,1)S(1)} collective-permute-done((bf16[128,1536]{1,0:T(8,128)(2,1)S(1)}, bf16[128,1536]{1,0:T(8,128)(2,1)S(1)}, u32[]{:S(2)}, u32[]{:S(2)}) %collective-permute-start.12) | collective-permute-done | bytes 393248 | tf_op jit(solution)/shard_map/ppermute | solution.py:36
  94.3 2.7 %collective-permute-done.11 = bf16[128,1536]{1,0:T(8,128)(2,1)S(1)} collective-permute-done((bf16[128,1536]{1,0:T(8,128)(2,1)S(1)}, bf16[128,1536]{1,0:T(8,128)(2,1)S(1)}, u32[]{:S(2)}, u32[]{:S(2)}) %collective-permute-start.11) | collective-permute-done | bytes 393248 | tf_op jit(solution)/shard_map/ppermute | solution.py:36
  97.0 9.8 %collective-permute-done.10 = bf16[128,1536]{1,0:T(8,128)(2,1)S(1)} collective-permute-done((bf16[128,1536]{1,0:T(8,128)(2,1)S(1)}, bf16[128,1536]{1,0:T(8,128)(2,1)S(1)}, u32[]{:S(2)}, u32[]{:S(2)}) %collective-permute-start.10) | collective-permute-done | bytes 393248 | tf_op jit(solution)/shard_map/ppermute | solution.py:36
  106.7 2.2 %multiply_convert_fusion = (bf16[128,1536]{1,0:T(8,128)(2,1)S(1)}, bf16[128,1536]{1,0:T(8,128)(2,1)S(1)}) fusion(bf16[128,1536]{1,0:T(8,128)(2,1)S(1)} %collective-permute-done.12, bf16[128,1536]{1,0:T(8,128)(2,1)S(1)} %collective-permute-done.11, bf16[128,1536]{1,0:T(8,128)(2,1)S(1)} %collective-permute-done.10, bf16[4,128,1536]{2,1,0:T(8,128)(2,1)} %bitcast.59, ...), kind=kLoop, calls=%fused_computation.31 | loop fusion | flops 6881280 | bytes 3932164 | tf_op jit(solution)/shard_map/convert_element_type | solution.py:293
  110.6 2.4 %constant_dynamic-slice_fusion.3 = (bf16[512,384]{1,0:T(8,128)(2,1)}, bf16[512,384]{1,0:T(8,128)(2,1)S(1)}, bf16[512,384]{1,0:T(8,128)(2,1)S(1)}, bf16[512,384]{1,0:T(8,128)(2,1)}) fusion(bf16[512,1536]{1,0:T(8,128)(2,1)} %all-gather.2.cloned.1.call-done, s32[]{:T(128)S(6)} %select_n.118, s32[]{:T(128)S(6)} %select_n.122, s32[]{:T(128)S(6)} %select_n.121, ...), kind=kLoop, calls=%fused_computation.47 | loop fusion | bytes 3145744 | tf_op jit(solution)/shard_map/dynamic_slice | solution.py:299
  113.0 6.2 %collective-permute-done.16.refs_1_ = bf16[128,1536]{1,0:T(8,128)(2,1)S(1)} collective-permute-done((bf16[128,1536]{1,0:T(8,128)(2,1)S(1)}, bf16[128,1536]{1,0:T(8,128)(2,1)S(1)}, u32[]{:S(2)}, u32[]{:S(2)}) %collective-permute-start.16) | collective-permute-done | bytes 393248 | tf_op jit(solution)/shard_map/ppermute | solution.py:36
  120.3 9.8 %collective-permute-done.18.refs_3_ = bf16[128,1536]{1,0:T(8,128)(2,1)S(1)} collective-permute-done((bf16[128,1536]{1,0:T(8,128)(2,1)S(1)}, bf16[128,1536]{1,0:T(8,128)(2,1)S(1)}, u32[]{:S(2)}, u32[]{:S(2)}) %collective-permute-start.18) | collective-permute-done | bytes 393248 | tf_op jit(solution)/shard_map/ppermute | solution.py:36
  131.5 2.8 %convolution_convert_fusion.1 = bf16[768,1536]{1,0:T(8,128)(2,1)} fusion(bf16[512,1536]{1,0:T(8,128)(2,1)S(1)} %put.6, bf16[512,384]{1,0:T(8,128)(2,1)S(1)} %get-tuple-element.46, bf16[512,384]{1,0:T(8,128)(2,1)S(1)} %get-tuple-element.47), kind=kOutput, calls=%fused_computation.2 | convolution fusion | flops 1210712064 | bytes 4718592 | tf_op jit(solution)/shard_map/dot_general | solution.py:40
  134.8 3.8 %convolution_convert_fusion.3 = bf16[512,1536]{1,0:T(8,128)(2,1)} fusion(bf16[512,1536]{1,0:T(8,128)(2,1)S(1)} %put.6, bf16[1536,1536]{1,0:T(8,128)(2,1)S(1)} %bitcast.56), kind=kOutput, calls=%fused_computation.4 | convolution fusion | flops 2416705536 | bytes 7864320 | tf_op jit(solution)/shard_map/dot_general | solution.py:40
  141.6 2.3 %add_convert_fusion = bf16[768,1536]{1,0:T(8,128)(2,1)S(1)} fusion(bf16[768,1536]{1,0:T(8,128)(2,1)} %collective-permute-done.19, bf16[768,1536]{1,0:T(8,128)(2,1)S(1)} %convolution_convert_fusion.2), kind=kLoop, calls=%fused_computation.1 | loop fusion | flops 4718592 | bytes 7077888 | tf_op jit(solution)/shard_map/convert_element_type | solution.py:307
  145.1 4.4 %collective-permute-done.20.refs_1_ = bf16[128,1536]{1,0:T(8,128)(2,1)S(1)} collective-permute-done((bf16[128,1536]{1,0:T(8,128)(2,1)S(1)}, bf16[128,1536]{1,0:T(8,128)(2,1)S(1)}, u32[]{:S(2)}, u32[]{:S(2)}) %collective-permute-start.20) | collective-permute-done | bytes 393248 | tf_op jit(solution)/shard_map/ppermute | solution.py:36
  151.4 9.1 %collective-permute-done.22.refs_3_ = bf16[128,1536]{1,0:T(8,128)(2,1)S(1)} collective-permute-done((bf16[128,1536]{1,0:T(8,128)(2,1)S(1)}, bf16[128,1536]{1,0:T(8,128)(2,1)S(1)}, u32[]{:S(2)}, u32[]{:S(2)}) %collective-permute-start.22) | collective-permute-done | bytes 393248 | tf_op jit(solution)/shard_map/ppermute | solution.py:36
  162.0 4.4 %convolution_convert_fusion = bf16[1536,1536]{1,0:T(8,128)(2,1)} fusion(bf16[512,1536]{1,0:T(8,128)(2,1)S(1)} %put.7, bf16[512,1536]{1,0:T(8,128)(2,1)S(1)} %copy-done.7), kind=kOutput, calls=%fused_computation | convolution fusion | flops 2418278400 | bytes 7864320 | tf_op jit(solution)/shard_map/dot_general | solution.py:40
  166.5 2.7 %collective-permute-start.24 = (bf16[384,1536]{1,0:T(8,128)(2,1)}, bf16[384,1536]{1,0:T(8,128)(2,1)}, u32[]{:S(2)}, u32[]{:S(2)}) collective-permute-start(bf16[384,1536]{1,0:T(8,128)(2,1)} %get-tuple-element.39), channel_id=1, source_target_pairs={{0,64},{32,96},{2,66},{34,98},{4,68},{36,100},{6,70},{38,102},{1,6... | collective-permute-start | bytes 3538952 | tf_op jit(solution)/shard_map/ppermute | solution.py:36
  169.3 4.9 %convolution_convert_fusion.4 = bf16[512,1536]{1,0:T(8,128)(2,1)S(1)} fusion(bf16[512,1536]{1,0:T(8,128)(2,1)S(1)} %put.7, bf16[1536,1536]{1,0:T(8,128)(2,1)} %copy-done.1), kind=kOutput, calls=%fused_computation.5 | convolution fusion | flops 2416705536 | bytes 7864320 | tf_op jit(solution)/shard_map/dot_general | solution.py:40
  178.4 19.2 %collective-permute-done.23 = bf16[128,1536]{1,0:T(8,128)(2,1)S(1)} collective-permute-done((bf16[128,1536]{1,0:T(8,128)(2,1)S(1)}, bf16[128,1536]{1,0:T(8,128)(2,1)S(1)}, u32[]{:S(2)}, u32[]{:S(2)}) %collective-permute-start.23) | collective-permute-done | bytes 393248 | tf_op jit(solution)/shard_map/ppermute | solution.py:36
  201.9 3.3 %copied.1.refs_4_ = bf16[384,3072]{1,0:T(8,128)(2,1)} custom-call(s32[6]{0:T(128)S(1)} %pad_add_fusion.4.refs_0_, bf16[384,1536]{1,0:T(8,128)(2,1)S(1)} %get-tuple-element.38.refs_1_, bf16[384,1536]{1,0:T(8,128)(2,1)} %collective-permute-done.24.refs_2_), custom_call_target="tpu_custom_call" | custom-call | flops 1024 | bytes 1024 | tf_op jit(solution)/shard_map/copied/pallas_call | solution.py:66
  206.8 2.9 %collective-permute-done.28.refs_2_ = bf16[64,1536]{1,0:T(8,128)(2,1)S(1)} collective-permute-done((bf16[64,1536]{1,0:T(8,128)(2,1)S(1)}, bf16[64,1536]{1,0:T(8,128)(2,1)S(1)}, u32[]{:S(2)}, u32[]{:S(2)}) %collective-permute-start.28) | collective-permute-done | bytes 196640 | tf_op jit(solution)/shard_map/ppermute | solution.py:36
  (103 shorter events, 46.1 us)
Async XLA Ops:
  7.2 69.5 %all-gather.2.cloned.1.call-start = ((), (), s32[]{:S(2)}) async-start(), calls=%async_computation.2 | async-start | bytes 1966080 | tf_op jit(solution)/shard_map/all_gather | solution.py:280
  7.2 18.7 %collective-permute-start.3 = (bf16[768,1536]{1,0:T(8,128)(2,1)}, bf16[768,1536]{1,0:T(8,128)(2,1)S(1)}, u32[]{:S(2)}, u32[]{:S(2)}) collective-permute-start(bf16[768,1536]{1,0:T(8,128)(2,1)} %refs_0_.1), channel_id=1, source_target_pairs={{0,32},{32,0},{2,34},{34,2},{4,36},{36,4},{6,38},{38,6},{1,33},{33... | collective-permute-start | bytes 7077896 | tf_op jit(solution)/shard_map/ppermute | solution.py:36
  10.5 11.2 %collective-permute-start = (bf16[64,1536]{1,0:T(8,128)(2,1)S(1)}, bf16[64,1536]{1,0:T(8,128)(2,1)S(1)}, u32[]{:S(2)}, u32[]{:S(2)}) collective-permute-start(bf16[64,1536]{1,0:T(8,128)(2,1)S(1)} %constant_dynamic-update-slice_fusion.refs_0_), channel_id=1, source_target_pairs={{0,65},{32,97},{2,67},{34,99},{4,69},{36,101},{6,71},{38,103},{1,0... | collective-permute-start | bytes 589832 | tf_op jit(solution)/shard_map/ppermute | solution.py:36
  13.3 8.4 %collective-permute-start.1 = (bf16[64,1536]{1,0:T(8,128)(2,1)S(1)}, bf16[64,1536]{1,0:T(8,128)(2,1)S(1)}, u32[]{:S(2)}, u32[]{:S(2)}) collective-permute-start(bf16[64,1536]{1,0:T(8,128)(2,1)S(1)} %constant_dynamic-update-slice_fusion.refs_0_), channel_id=1, source_target_pairs={{0,64},{32,96},{2,66},{34,98},{4,68},{36,100},{6,70},{38,102},{1,6... | collective-permute-start | bytes 589832 | tf_op jit(solution)/shard_map/ppermute | solution.py:36
  13.7 12.2 %collective-permute-start.2 = (bf16[64,1536]{1,0:T(8,128)(2,1)S(1)}, bf16[64,1536]{1,0:T(8,128)(2,1)S(1)}, u32[]{:S(2)}, u32[]{:S(2)}) collective-permute-start(bf16[64,1536]{1,0:T(8,128)(2,1)S(1)} %constant_dynamic-update-slice_fusion.refs_0_), channel_id=1, source_target_pairs={{0,1},{32,33},{2,3},{34,35},{4,5},{36,37},{6,7},{38,39},{1,64},{33... | collective-permute-start | bytes 589832 | tf_op jit(solution)/shard_map/ppermute | solution.py:36
  28.4 20.3 %collective-permute-start.4 = (bf16[128,1536]{1,0:T(8,128)(2,1)}, bf16[128,1536]{1,0:T(8,128)(2,1)}, u32[]{:S(2)}, u32[]{:S(2)}) collective-permute-start(bf16[128,1536]{1,0:T(8,128)(2,1)} %get-tuple-element.21.refs_0_), channel_id=1, source_target_pairs={{0,6},{32,38},{2,0},{34,32},{4,2},{36,34},{6,4},{38,36},{1,7},{33,... | collective-permute-start | bytes 1179656 | tf_op jit(solution)/shard_map/ppermute | solution.py:36
  32.2 16.6 %collective-permute-start.5 = (bf16[128,1536]{1,0:T(8,128)(2,1)}, bf16[128,1536]{1,0:T(8,128)(2,1)}, u32[]{:S(2)}, u32[]{:S(2)}) collective-permute-start(bf16[128,1536]{1,0:T(8,128)(2,1)} %get-tuple-element.21.refs_0_), channel_id=1, source_target_pairs={{0,4},{32,36},{2,6},{34,38},{4,0},{36,32},{6,2},{38,34},{1,5},{33,... | collective-permute-start | bytes 1179656 | tf_op jit(solution)/shard_map/ppermute | solution.py:36
  32.2 20.7 %collective-permute-start.6 = (bf16[128,1536]{1,0:T(8,128)(2,1)}, bf16[128,1536]{1,0:T(8,128)(2,1)}, u32[]{:S(2)}, u32[]{:S(2)}) collective-permute-start(bf16[128,1536]{1,0:T(8,128)(2,1)} %get-tuple-element.21.refs_0_), channel_id=1, source_target_pairs={{0,2},{32,34},{2,4},{34,36},{4,6},{36,38},{6,0},{38,32},{1,3},{33,... | collective-permute-start | bytes 1179656 | tf_op jit(solution)/shard_map/ppermute | solution.py:36
  35.7 29.1 %collective-permute-start.7 = (bf16[384,1536]{1,0:T(8,128)(2,1)}, bf16[384,1536]{1,0:T(8,128)(2,1)}, u32[]{:S(2)}, u32[]{:S(2)}) collective-permute-start(bf16[384,1536]{1,0:T(8,128)(2,1)} %get-tuple-element.23), channel_id=1, source_target_pairs={{0,64},{32,96},{2,66},{34,98},{4,68},{36,100},{6,70},{38,102},{1,6... | collective-permute-start | bytes 3538952 | tf_op jit(solution)/shard_map/ppermute | solution.py:36
  52.9 124.4 %reduce-scatter.3.cloned.1.call-start = ((), (), s32[]{:S(2)}) async-start(), calls=%async_computation.3 | async-start | bytes 1966080 | tf_op jit(solution)/shard_map/reduce_scatter | solution.py:306
  52.9 16.6 %collective-permute-start.8 = (bf16[384,1536]{1,0:T(8,128)(2,1)S(1)}, bf16[384,1536]{1,0:T(8,128)(2,1)}, u32[]{:S(2)}, u32[]{:S(2)}) collective-permute-start(bf16[384,1536]{1,0:T(8,128)(2,1)S(1)} %get-tuple-element.41.refs_0_), channel_id=1, source_target_pairs={{0,32},{32,0},{2,34},{34,2},{4,36},{36,4},{6,38},{38,6},{1,33},{33... | collective-permute-start | bytes 3538952 | tf_op jit(solution)/shard_map/ppermute | solution.py:36
  66.0 20.4 %collective-permute-start.15 = (bf16[128,1536]{1,0:T(8,128)(2,1)}, bf16[128,1536]{1,0:T(8,128)(2,1)}, u32[]{:S(2)}, u32[]{:S(2)}) collective-permute-start(bf16[128,1536]{1,0:T(8,128)(2,1)} %copy-done.5), channel_id=1, source_target_pairs={{0,24},{32,56},{2,26},{34,58},{4,28},{36,60},{6,30},{38,62},{1,25}... | collective-permute-start | bytes 1179656 | tf_op jit(solution)/shard_map/ppermute | solution.py:36
  68.5 18.5 %collective-permute-start.14 = (bf16[128,1536]{1,0:T(8,128)(2,1)S(1)}, bf16[128,1536]{1,0:T(8,128)(2,1)}, u32[]{:S(2)}, u32[]{:S(2)}) collective-permute-start(bf16[128,1536]{1,0:T(8,128)(2,1)S(1)} %get-tuple-element.27), channel_id=1, source_target_pairs={{0,16},{32,48},{2,18},{34,50},{4,20},{36,52},{6,22},{38,54},{1,17}... | collective-permute-start | bytes 1179656 | tf_op jit(solution)/shard_map/ppermute | solution.py:36
  69.0 20.6 %collective-permute-start.13 = (bf16[128,1536]{1,0:T(8,128)(2,1)S(1)}, bf16[128,1536]{1,0:T(8,128)(2,1)}, u32[]{:S(2)}, u32[]{:S(2)}) collective-permute-start(bf16[128,1536]{1,0:T(8,128)(2,1)S(1)} %get-tuple-element.26), channel_id=1, source_target_pairs={{0,8},{32,40},{2,10},{34,42},{4,12},{36,44},{6,14},{38,46},{1,9},{... | collective-permute-start | bytes 1179656 | tf_op jit(solution)/shard_map/ppermute | solution.py:36
  83.3 11.0 %collective-permute-start.12 = (bf16[128,1536]{1,0:T(8,128)(2,1)S(1)}, bf16[128,1536]{1,0:T(8,128)(2,1)S(1)}, u32[]{:S(2)}, u32[]{:S(2)}) collective-permute-start(bf16[128,1536]{1,0:T(8,128)(2,1)S(1)} %get-tuple-element.50), channel_id=1, source_target_pairs={{0,24},{32,56},{2,26},{34,58},{4,28},{36,60},{6,30},{38,62},{1,25}... | collective-permute-start | bytes 1179656 | tf_op jit(solution)/shard_map/ppermute | solution.py:36
  85.8 11.2 %collective-permute-start.11 = (bf16[128,1536]{1,0:T(8,128)(2,1)S(1)}, bf16[128,1536]{1,0:T(8,128)(2,1)S(1)}, u32[]{:S(2)}, u32[]{:S(2)}) collective-permute-start(bf16[128,1536]{1,0:T(8,128)(2,1)S(1)} %get-tuple-element.51), channel_id=1, source_target_pairs={{0,16},{32,48},{2,18},{34,50},{4,20},{36,52},{6,22},{38,54},{1,17}... | collective-permute-start | bytes 1179656 | tf_op jit(solution)/shard_map/ppermute | solution.py:36
  86.3 20.4 %collective-permute-start.10 = (bf16[128,1536]{1,0:T(8,128)(2,1)S(1)}, bf16[128,1536]{1,0:T(8,128)(2,1)S(1)}, u32[]{:S(2)}, u32[]{:S(2)}) collective-permute-start(bf16[128,1536]{1,0:T(8,128)(2,1)S(1)} %get-tuple-element.49), channel_id=1, source_target_pairs={{0,8},{32,40},{2,10},{34,42},{4,12},{36,44},{6,14},{38,46},{1,9},{... | collective-permute-start | bytes 1179656 | tf_op jit(solution)/shard_map/ppermute | solution.py:36
  109.0 10.3 %collective-permute-start.16 = (bf16[128,1536]{1,0:T(8,128)(2,1)S(1)}, bf16[128,1536]{1,0:T(8,128)(2,1)S(1)}, u32[]{:S(2)}, u32[]{:S(2)}) collective-permute-start(bf16[128,1536]{1,0:T(8,128)(2,1)S(1)} %get-tuple-element.37.refs_0_), channel_id=1, source_target_pairs={{0,24},{32,56},{2,26},{34,58},{4,28},{36,60},{6,30},{38,62},{1,25}... | collective-permute-start | bytes 1179656 | tf_op jit(solution)/shard_map/ppermute | solution.py:36
  109.1 11.2 %collective-permute-start.17 = (bf16[128,1536]{1,0:T(8,128)(2,1)S(1)}, bf16[128,1536]{1,0:T(8,128)(2,1)S(1)}, u32[]{:S(2)}, u32[]{:S(2)}) collective-permute-start(bf16[128,1536]{1,0:T(8,128)(2,1)S(1)} %get-tuple-element.37.refs_0_), channel_id=1, source_target_pairs={{0,16},{32,48},{2,18},{34,50},{4,20},{36,52},{6,22},{38,54},{1,17}... | collective-permute-start | bytes 1179656 | tf_op jit(solution)/shard_map/ppermute | solution.py:36
  109.7 20.4 %collective-permute-start.18 = (bf16[128,1536]{1,0:T(8,128)(2,1)S(1)}, bf16[128,1536]{1,0:T(8,128)(2,1)S(1)}, u32[]{:S(2)}, u32[]{:S(2)}) collective-permute-start(bf16[128,1536]{1,0:T(8,128)(2,1)S(1)} %get-tuple-element.37.refs_0_), channel_id=1, source_target_pairs={{0,8},{32,40},{2,10},{34,42},{4,12},{36,44},{6,14},{38,46},{1,9},{... | collective-permute-start | bytes 1179656 | tf_op jit(solution)/shard_map/ppermute | solution.py:36
  134.3 7.3 %collective-permute-start.19 = (bf16[768,1536]{1,0:T(8,128)(2,1)}, bf16[768,1536]{1,0:T(8,128)(2,1)}, u32[]{:S(2)}, u32[]{:S(2)}) collective-permute-start(bf16[768,1536]{1,0:T(8,128)(2,1)} %convolution_convert_fusion.1), channel_id=1, source_target_pairs={{0,32},{32,0},{2,34},{34,2},{4,36},{36,4},{6,38},{38,6},{1,33},{33... | collective-permute-start | bytes 7077896 | tf_op jit(solution)/shard_map/ppermute | solution.py:36
  138.6 74.6 %reduce-scatter.5.cloned.1.call-start = ((), (), s32[]{:S(2)}) async-start(), calls=%async_computation.4 | async-start | bytes 7077888 | tf_op jit(solution)/shard_map/reduce_scatter | solution.py:313
  138.6 10.9 %collective-permute-start.20 = (bf16[128,1536]{1,0:T(8,128)(2,1)S(1)}, bf16[128,1536]{1,0:T(8,128)(2,1)S(1)}, u32[]{:S(2)}, u32[]{:S(2)}) collective-permute-start(bf16[128,1536]{1,0:T(8,128)(2,1)S(1)} %get-tuple-element.30.refs_0_), channel_id=1, source_target_pairs={{0,24},{32,56},{2,26},{34,58},{4,28},{36,60},{6,30},{38,62},{1,25}... | collective-permute-start | bytes 1179656 | tf_op jit(solution)/shard_map/ppermute | solution.py:36
  139.5 11.9 %collective-permute-start.21 = (bf16[128,1536]{1,0:T(8,128)(2,1)S(1)}, bf16[128,1536]{1,0:T(8,128)(2,1)S(1)}, u32[]{:S(2)}, u32[]{:S(2)}) collective-permute-start(bf16[128,1536]{1,0:T(8,128)(2,1)S(1)} %get-tuple-element.30.refs_0_), channel_id=1, source_target_pairs={{0,16},{32,48},{2,18},{34,50},{4,20},{36,52},{6,22},{38,54},{1,17}... | collective-permute-start | bytes 1179656 | tf_op jit(solution)/shard_map/ppermute | solution.py:36
  139.6 21.0 %collective-permute-start.22 = (bf16[128,1536]{1,0:T(8,128)(2,1)S(1)}, bf16[128,1536]{1,0:T(8,128)(2,1)S(1)}, u32[]{:S(2)}, u32[]{:S(2)}) collective-permute-start(bf16[128,1536]{1,0:T(8,128)(2,1)S(1)} %get-tuple-element.30.refs_0_), channel_id=1, source_target_pairs={{0,8},{32,40},{2,10},{34,42},{4,12},{36,44},{6,14},{38,46},{1,9},{... | collective-permute-start | bytes 1179656 | tf_op jit(solution)/shard_map/ppermute | solution.py:36
  166.5 31.1 %collective-permute-start.24 = (bf16[384,1536]{1,0:T(8,128)(2,1)}, bf16[384,1536]{1,0:T(8,128)(2,1)}, u32[]{:S(2)}, u32[]{:S(2)}) collective-permute-start(bf16[384,1536]{1,0:T(8,128)(2,1)} %get-tuple-element.39), channel_id=1, source_target_pairs={{0,64},{32,96},{2,66},{34,98},{4,68},{36,100},{6,70},{38,102},{1,6... | collective-permute-start | bytes 3538952 | tf_op jit(solution)/shard_map/ppermute | solution.py:36
  175.5 22.1 %collective-permute-start.26 = (bf16[128,1536]{1,0:T(8,128)(2,1)S(1)}, bf16[128,1536]{1,0:T(8,128)(2,1)S(1)}, u32[]{:S(2)}, u32[]{:S(2)}) collective-permute-start(bf16[128,1536]{1,0:T(8,128)(2,1)S(1)} %get-tuple-element.43), channel_id=1, source_target_pairs={{0,6},{32,38},{2,0},{34,32},{4,2},{36,34},{6,4},{38,36},{1,7},{33,... | collective-permute-start | bytes 1179656 | tf_op jit(solution)/shard_map/ppermute | solution.py:36
  176.6 21.0 %collective-permute-start.25 = (bf16[128,1536]{1,0:T(8,128)(2,1)S(1)}, bf16[128,1536]{1,0:T(8,128)(2,1)S(1)}, u32[]{:S(2)}, u32[]{:S(2)}) collective-permute-start(bf16[128,1536]{1,0:T(8,128)(2,1)S(1)} %get-tuple-element.44), channel_id=1, source_target_pairs={{0,4},{32,36},{2,6},{34,38},{4,0},{36,32},{6,2},{38,34},{1,5},{33,... | collective-permute-start | bytes 1179656 | tf_op jit(solution)/shard_map/ppermute | solution.py:36
  177.3 20.3 %collective-permute-start.23 = (bf16[128,1536]{1,0:T(8,128)(2,1)S(1)}, bf16[128,1536]{1,0:T(8,128)(2,1)S(1)}, u32[]{:S(2)}, u32[]{:S(2)}) collective-permute-start(bf16[128,1536]{1,0:T(8,128)(2,1)S(1)} %get-tuple-element.42), channel_id=1, source_target_pairs={{0,2},{32,34},{2,4},{34,36},{4,6},{36,38},{6,0},{38,32},{1,3},{33,... | collective-permute-start | bytes 1179656 | tf_op jit(solution)/shard_map/ppermute | solution.py:36
  198.9 7.9 %collective-permute-start.27 = (bf16[64,1536]{1,0:T(8,128)(2,1)S(1)}, bf16[64,1536]{1,0:T(8,128)(2,1)S(1)}, u32[]{:S(2)}, u32[]{:S(2)}) collective-permute-start(bf16[64,1536]{1,0:T(8,128)(2,1)S(1)} %pad_maximum_fusion.1), channel_id=1, source_target_pairs={{0,1},{32,33},{2,3},{34,35},{4,5},{36,37},{6,7},{38,39},{1,64},{33... | collective-permute-start | bytes 589832 | tf_op jit(solution)/shard_map/ppermute | solution.py:36
  199.3 10.4 %collective-permute-start.28 = (bf16[64,1536]{1,0:T(8,128)(2,1)S(1)}, bf16[64,1536]{1,0:T(8,128)(2,1)S(1)}, u32[]{:S(2)}, u32[]{:S(2)}) collective-permute-start(bf16[64,1536]{1,0:T(8,128)(2,1)S(1)} %pad_maximum_fusion.2), channel_id=1, source_target_pairs={{0,64},{32,96},{2,66},{34,98},{4,68},{36,100},{6,70},{38,102},{1,6... | collective-permute-start | bytes 589832 | tf_op jit(solution)/shard_map/ppermute | solution.py:36
  201.2 9.6 %collective-permute-start.29 = (bf16[64,1536]{1,0:T(8,128)(2,1)S(1)}, bf16[64,1536]{1,0:T(8,128)(2,1)S(1)}, u32[]{:S(2)}, u32[]{:S(2)}) collective-permute-start(bf16[64,1536]{1,0:T(8,128)(2,1)S(1)} %pad_maximum_fusion.3), channel_id=1, source_target_pairs={{0,65},{32,97},{2,67},{34,99},{4,69},{36,101},{6,71},{38,103},{1,0... | collective-permute-start | bytes 589832 | tf_op jit(solution)/shard_map/ppermute | solution.py:36
  (15 other events, 34.3 us)
Sparse Core Ops, SparseCore 0:
  53.0 23.5 all-gather.1
  138.7 22.1 reduce-scatter.2
  166.5 13.3 reduce-scatter.4

commit v2 on v1

--- a/solution.py
+++ b/solution.py
@@ -315,7 +315,7 @@
     out_rows = total(out_terms).astype(BF16)
     grad_w_in = copied((384, 2 * units), [(kept, 0, 0, b), (arrived, 0, 0, 1 - b)])
     parts = [jnp.concatenate([v[i * 32 : (i + 1) * 32] for v in (out_rows, in_rows)]) for i in range(4)]
-    return (*last(scatter(parts, "dy"), [grad_w_in]), grad_w_in, grad_w_out)
+    return (*last(scatter(parts, "dy"), []), grad_w_in, grad_w_out)
 
 
 def solution(mesh):

time: 221 us -> 219 us (level)
    unnamed x29 -> x27, local copies, waits for them, and re-layouts: 11.5 us -> 9.76 us
where the time goes in v2:
time: 219 us; the launch traced here: 218 us
  waiting for transfers between devices  108 us (49%)
  starting transfers between devices  30.6 us (14%)
  matrix products  22.7 us (10%)
  local copies, waits for them, and re-layouts  18.3 us (8%)
  Pallas kernels  18.2 us (8%)
  between operations  14.1 us (6%)
  other arithmetic  6.17 us (3%)
    ppermute x30, waiting for transfers between devices, shift(): return lax.ppermute(value, AXES, pairs)  105 us
    ppermute x30, starting transfers between devices, shift(): return lax.ppermute(value, AXES, pairs)  30.5 us
    dot_general x6, matrix products, mul(): lax.dot_general(left, right, dims, preferred_element_type=F32).astype(BF16)  22.7 us
    unnamed x27, local copies, waits for them, and re-layouts  9.76 us
    pallas_call x1, Pallas kernels, product(): pl.pallas_call(kernel, grid=(1536 // wide,), out_shape=out_shape, in_spec...  6.29 us
    pallas_call x4, Pallas kernels, put(): pl.pallas_call(kernel, out_shape=[jax.ShapeDtypeStruct((n * rows, width),...  6.04 us
    pallas_call x3, Pallas kernels, call(): pl.pallas_call(waiting, grid=grid, out_shape=[jax.ShapeDtypeStruct(shape,...  5.89 us
  transfers between devices with their start and end apart: 33, of which 19 were waited for; matrix products, arithmetic and copies ran while one was open for 15% of the time, Pallas kernels for 7%

profile of v2, /device:TPU:1, one launch (start us, length us, event | category | flops | bytes accessed | tf_op | source)
XLA Modules:
  0.0 218.1 jit_solution(12763394112490362772)
XLA Ops:
  10.5 2.8 %collective-permute-start = (bf16[64,1536]{1,0:T(8,128)(2,1)S(1)}, bf16[64,1536]{1,0:T(8,128)(2,1)S(1)}, u32[]{:S(2)}, u32[]{:S(2)}) collective-permute-start(bf16[64,1536]{1,0:T(8,128)(2,1)S(1)} %constant_dynamic-update-slice_fusion.refs_0_), channel_id=1, source_target_pairs={{0,65},{32,97},{2,67},{34,99},{4,69},{36,101},{6,71},{38,103},{1,0... | collective-permute-start | bytes 589832 | tf_op jit(solution)/shard_map/ppermute | solution.py:36
  14.4 7.3 %collective-permute-done.refs_1_ = bf16[64,1536]{1,0:T(8,128)(2,1)S(1)} collective-permute-done((bf16[64,1536]{1,0:T(8,128)(2,1)S(1)}, bf16[64,1536]{1,0:T(8,128)(2,1)S(1)}, u32[]{:S(2)}, u32[]{:S(2)}) %collective-permute-start) | collective-permute-done | bytes 196640 | tf_op jit(solution)/shard_map/ppermute | solution.py:36
  21.7 4.1 %collective-permute-done.2.refs_3_ = bf16[64,1536]{1,0:T(8,128)(2,1)S(1)} collective-permute-done((bf16[64,1536]{1,0:T(8,128)(2,1)S(1)}, bf16[64,1536]{1,0:T(8,128)(2,1)S(1)}, u32[]{:S(2)}, u32[]{:S(2)}) %collective-permute-start.2) | collective-permute-done | bytes 196640 | tf_op jit(solution)/shard_map/ppermute | solution.py:36
  28.4 3.8 %collective-permute-start.4 = (bf16[128,1536]{1,0:T(8,128)(2,1)}, bf16[128,1536]{1,0:T(8,128)(2,1)}, u32[]{:S(2)}, u32[]{:S(2)}) collective-permute-start(bf16[128,1536]{1,0:T(8,128)(2,1)} %get-tuple-element.21.refs_0_), channel_id=1, source_target_pairs={{0,6},{32,38},{2,0},{34,32},{4,2},{36,34},{6,4},{38,36},{1,7},{33,... | collective-permute-start | bytes 1179656 | tf_op jit(solution)/shard_map/ppermute | solution.py:36
  32.9 2.8 %constant_dynamic-slice_fusion.4 = (bf16[384,1536]{1,0:T(8,128)(2,1)}, bf16[384,1536]{1,0:T(8,128)(2,1)S(1)}) fusion(bf16[384,3072]{1,0:T(8,128)(2,1)} %param.5, s32[]{:T(128)S(6)} %select_n.106, s32[]{:T(128)S(6)} %select_n.105), kind=kLoop, calls=%fused_computation.48 | loop fusion | bytes 4718600 | tf_op jit(solution)/shard_map/dynamic_slice | solution.py:274
  36.0 12.7 %collective-permute-done.4.refs_1_ = bf16[128,1536]{1,0:T(8,128)(2,1)} collective-permute-done((bf16[128,1536]{1,0:T(8,128)(2,1)}, bf16[128,1536]{1,0:T(8,128)(2,1)}, u32[]{:S(2)}, u32[]{:S(2)}) %collective-permute-start.4) | collective-permute-done | bytes 393248 | tf_op jit(solution)/shard_map/ppermute | solution.py:36
  48.8 4.1 %collective-permute-done.6.refs_3_ = bf16[128,1536]{1,0:T(8,128)(2,1)} collective-permute-done((bf16[128,1536]{1,0:T(8,128)(2,1)}, bf16[128,1536]{1,0:T(8,128)(2,1)}, u32[]{:S(2)}, u32[]{:S(2)}) %collective-permute-start.6) | collective-permute-done | bytes 393248 | tf_op jit(solution)/shard_map/ppermute | solution.py:36
  56.6 6.3 %product.1 = (bf16[128,1536]{1,0:T(8,128)(2,1)S(1)}, bf16[128,1536]{1,0:T(8,128)(2,1)S(1)}, bf16[128,1536]{1,0:T(8,128)(2,1)S(1)}, bf16[128,1536]{1,0:T(8,128)(2,1)S(1)}, bf16[512,1536]{1,0:T(8,128)(2,1)S(1)}) custom-call(s32[4]{0:T(128)S(1)} %pad_add_fusion.1.place_ref, bf16[128,1536]{1,0:T(8,128)(2,1)} %get-tuple-element.21.refs_0_, ...), custom_call_target="tpu_custom_call" | custom-call | flops 2415919104 | bytes 8388608 | tf_op jit(solution)/shard_map/product/pallas_call | solution.py:220
  66.0 2.5 %collective-permute-start.15 = (bf16[128,1536]{1,0:T(8,128)(2,1)}, bf16[128,1536]{1,0:T(8,128)(2,1)}, u32[]{:S(2)}, u32[]{:S(2)}) collective-permute-start(bf16[128,1536]{1,0:T(8,128)(2,1)} %copy-done.4), channel_id=1, source_target_pairs={{0,24},{32,56},{2,26},{34,58},{4,28},{36,60},{6,30},{38,62},{1,25}... | collective-permute-start | bytes 1179656 | tf_op jit(solution)/shard_map/ppermute | solution.py:36
  69.6 2.5 %put.5 = bf16[1536,1536]{1,0:T(8,128)(2,1)S(1)} custom-call(s32[4]{0:T(128)S(1)} %pad_add_fusion.index_ref, bf16[384,1536]{1,0:T(8,128)(2,1)S(1)} %get-tuple-element.41.refs_0_, bf16[384,1536]{1,0:T(8,128)(2,1)} %collective-permute-done.7.refs_1_, bf16[384,1536]{1,0:T(8,128)(2,1)} %collective-permute-done.8.refs_2_, ...), custom_call_target="tpu_custom_call" | custom-call | tf_op jit(solution)/shard_map/put/pallas_call | solution.py:171
  74.3 2.4 %all-gather.2.cloned.1.call-done = bf16[512,1536]{1,0:T(8,128)(2,1)} async-done(((bf16[128,1536]{1,0:T(8,128)(2,1)}), bf16[512,1536]{1,0:T(8,128)(2,1)}) %all-gather.2.cloned.1.call-update) | async-done | bytes 1572880 | tf_op jit(solution)/shard_map/all_gather | solution.py:280
  76.6 5.4 %convolution_convert_fusion.5 = bf16[512,1536]{1,0:T(8,128)(2,1)S(1)} fusion(bf16[512,1536]{1,0:T(8,128)(2,1)} %all-gather.2.cloned.1.call-done, bf16[1536,1536]{1,0:T(8,128)(2,1)} %copy-done.1), kind=kOutput, calls=%fused_computation.6 | convolution fusion | flops 2416705536 | bytes 7864320 | tf_op jit(solution)/shard_map/dot_general | solution.py:40
  83.3 2.5 %collective-permute-start.12 = (bf16[128,1536]{1,0:T(8,128)(2,1)S(1)}, bf16[128,1536]{1,0:T(8,128)(2,1)S(1)}, u32[]{:S(2)}, u32[]{:S(2)}) collective-permute-start(bf16[128,1536]{1,0:T(8,128)(2,1)S(1)} %get-tuple-element.50), channel_id=1, source_target_pairs={{0,24},{32,56},{2,26},{34,58},{4,28},{36,60},{6,30},{38,62},{1,25}... | collective-permute-start | bytes 1179656 | tf_op jit(solution)/shard_map/ppermute | solution.py:36
  86.9 2.6 %collective-permute-done.13 = bf16[128,1536]{1,0:T(8,128)(2,1)} collective-permute-done((bf16[128,1536]{1,0:T(8,128)(2,1)S(1)}, bf16[128,1536]{1,0:T(8,128)(2,1)}, u32[]{:S(2)}, u32[]{:S(2)}) %collective-permute-start.13) | collective-permute-done | bytes 393248 | tf_op jit(solution)/shard_map/ppermute | solution.py:36
  89.5 4.7 %collective-permute-done.12 = bf16[128,1536]{1,0:T(8,128)(2,1)S(1)} collective-permute-done((bf16[128,1536]{1,0:T(8,128)(2,1)S(1)}, bf16[128,1536]{1,0:T(8,128)(2,1)S(1)}, u32[]{:S(2)}, u32[]{:S(2)}) %collective-permute-start.12) | collective-permute-done | bytes 393248 | tf_op jit(solution)/shard_map/ppermute | solution.py:36
  94.3 2.7 %collective-permute-done.11 = bf16[128,1536]{1,0:T(8,128)(2,1)S(1)} collective-permute-done((bf16[128,1536]{1,0:T(8,128)(2,1)S(1)}, bf16[128,1536]{1,0:T(8,128)(2,1)S(1)}, u32[]{:S(2)}, u32[]{:S(2)}) %collective-permute-start.11) | collective-permute-done | bytes 393248 | tf_op jit(solution)/shard_map/ppermute | solution.py:36
  97.0 9.8 %collective-permute-done.10 = bf16[128,1536]{1,0:T(8,128)(2,1)S(1)} collective-permute-done((bf16[128,1536]{1,0:T(8,128)(2,1)S(1)}, bf16[128,1536]{1,0:T(8,128)(2,1)S(1)}, u32[]{:S(2)}, u32[]{:S(2)}) %collective-permute-start.10) | collective-permute-done | bytes 393248 | tf_op jit(solution)/shard_map/ppermute | solution.py:36
  106.7 2.2 %multiply_convert_fusion = (bf16[128,1536]{1,0:T(8,128)(2,1)S(1)}, bf16[128,1536]{1,0:T(8,128)(2,1)S(1)}) fusion(bf16[128,1536]{1,0:T(8,128)(2,1)S(1)} %collective-permute-done.12, bf16[128,1536]{1,0:T(8,128)(2,1)S(1)} %collective-permute-done.11, bf16[128,1536]{1,0:T(8,128)(2,1)S(1)} %collective-permute-done.10, bf16[4,128,1536]{2,1,0:T(8,128)(2,1)} %bitcast.59, ...), kind=kLoop, calls=%fused_computation.31 | loop fusion | flops 6881280 | bytes 3932164 | tf_op jit(solution)/shard_map/convert_element_type | solution.py:293
  110.6 2.4 %constant_dynamic-slice_fusion.3 = (bf16[512,384]{1,0:T(8,128)(2,1)}, bf16[512,384]{1,0:T(8,128)(2,1)S(1)}, bf16[512,384]{1,0:T(8,128)(2,1)S(1)}, bf16[512,384]{1,0:T(8,128)(2,1)}) fusion(bf16[512,1536]{1,0:T(8,128)(2,1)} %all-gather.2.cloned.1.call-done, s32[]{:T(128)S(6)} %select_n.118, s32[]{:T(128)S(6)} %select_n.122, s32[]{:T(128)S(6)} %select_n.121, ...), kind=kLoop, calls=%fused_computation.47 | loop fusion | bytes 3145744 | tf_op jit(solution)/shard_map/dynamic_slice | solution.py:299
  113.0 6.2 %collective-permute-done.16.refs_1_ = bf16[128,1536]{1,0:T(8,128)(2,1)S(1)} collective-permute-done((bf16[128,1536]{1,0:T(8,128)(2,1)S(1)}, bf16[128,1536]{1,0:T(8,128)(2,1)S(1)}, u32[]{:S(2)}, u32[]{:S(2)}) %collective-permute-start.16) | collective-permute-done | bytes 393248 | tf_op jit(solution)/shard_map/ppermute | solution.py:36
  120.3 9.8 %collective-permute-done.18.refs_3_ = bf16[128,1536]{1,0:T(8,128)(2,1)S(1)} collective-permute-done((bf16[128,1536]{1,0:T(8,128)(2,1)S(1)}, bf16[128,1536]{1,0:T(8,128)(2,1)S(1)}, u32[]{:S(2)}, u32[]{:S(2)}) %collective-permute-start.18) | collective-permute-done | bytes 393248 | tf_op jit(solution)/shard_map/ppermute | solution.py:36
  131.5 2.8 %convolution_convert_fusion.1 = bf16[768,1536]{1,0:T(8,128)(2,1)} fusion(bf16[512,1536]{1,0:T(8,128)(2,1)S(1)} %put.6, bf16[512,384]{1,0:T(8,128)(2,1)S(1)} %get-tuple-element.46, bf16[512,384]{1,0:T(8,128)(2,1)S(1)} %get-tuple-element.47), kind=kOutput, calls=%fused_computation.2 | convolution fusion | flops 1210712064 | bytes 4718592 | tf_op jit(solution)/shard_map/dot_general | solution.py:40
  134.8 3.8 %convolution_convert_fusion.3 = bf16[512,1536]{1,0:T(8,128)(2,1)} fusion(bf16[512,1536]{1,0:T(8,128)(2,1)S(1)} %put.6, bf16[1536,1536]{1,0:T(8,128)(2,1)S(1)} %bitcast.56), kind=kOutput, calls=%fused_computation.4 | convolution fusion | flops 2416705536 | bytes 7864320 | tf_op jit(solution)/shard_map/dot_general | solution.py:40
  141.6 2.3 %add_convert_fusion = bf16[768,1536]{1,0:T(8,128)(2,1)S(1)} fusion(bf16[768,1536]{1,0:T(8,128)(2,1)} %collective-permute-done.19, bf16[768,1536]{1,0:T(8,128)(2,1)S(1)} %convolution_convert_fusion.2), kind=kLoop, calls=%fused_computation.1 | loop fusion | flops 4718592 | bytes 7077888 | tf_op jit(solution)/shard_map/convert_element_type | solution.py:307
  145.1 4.5 %collective-permute-done.20.refs_1_ = bf16[128,1536]{1,0:T(8,128)(2,1)S(1)} collective-permute-done((bf16[128,1536]{1,0:T(8,128)(2,1)S(1)}, bf16[128,1536]{1,0:T(8,128)(2,1)S(1)}, u32[]{:S(2)}, u32[]{:S(2)}) %collective-permute-start.20) | collective-permute-done | bytes 393248 | tf_op jit(solution)/shard_map/ppermute | solution.py:36
  151.4 9.2 %collective-permute-done.22.refs_3_ = bf16[128,1536]{1,0:T(8,128)(2,1)S(1)} collective-permute-done((bf16[128,1536]{1,0:T(8,128)(2,1)S(1)}, bf16[128,1536]{1,0:T(8,128)(2,1)S(1)}, u32[]{:S(2)}, u32[]{:S(2)}) %collective-permute-start.22) | collective-permute-done | bytes 393248 | tf_op jit(solution)/shard_map/ppermute | solution.py:36
  162.0 4.4 %convolution_convert_fusion = bf16[1536,1536]{1,0:T(8,128)(2,1)} fusion(bf16[512,1536]{1,0:T(8,128)(2,1)S(1)} %put.7, bf16[512,1536]{1,0:T(8,128)(2,1)S(1)} %copy-done.6), kind=kOutput, calls=%fused_computation | convolution fusion | flops 2418278400 | bytes 7864320 | tf_op jit(solution)/shard_map/dot_general | solution.py:40
  166.5 2.8 %collective-permute-start.24 = (bf16[384,1536]{1,0:T(8,128)(2,1)}, bf16[384,1536]{1,0:T(8,128)(2,1)}, u32[]{:S(2)}, u32[]{:S(2)}) collective-permute-start(bf16[384,1536]{1,0:T(8,128)(2,1)} %get-tuple-element.39), channel_id=1, source_target_pairs={{0,64},{32,96},{2,66},{34,98},{4,68},{36,100},{6,70},{38,102},{1,6... | collective-permute-start | bytes 3538952 | tf_op jit(solution)/shard_map/ppermute | solution.py:36
  169.3 4.9 %convolution_convert_fusion.4 = bf16[512,1536]{1,0:T(8,128)(2,1)S(1)} fusion(bf16[512,1536]{1,0:T(8,128)(2,1)S(1)} %put.7, bf16[1536,1536]{1,0:T(8,128)(2,1)} %copy-done), kind=kOutput, calls=%fused_computation.5 | convolution fusion | flops 2416705536 | bytes 7864320 | tf_op jit(solution)/shard_map/dot_general | solution.py:40
  178.4 19.2 %collective-permute-done.23 = bf16[128,1536]{1,0:T(8,128)(2,1)S(1)} collective-permute-done((bf16[128,1536]{1,0:T(8,128)(2,1)S(1)}, bf16[128,1536]{1,0:T(8,128)(2,1)S(1)}, u32[]{:S(2)}, u32[]{:S(2)}) %collective-permute-start.23) | collective-permute-done | bytes 393248 | tf_op jit(solution)/shard_map/ppermute | solution.py:36
  201.9 3.3 %copied.1 = bf16[384,3072]{1,0:T(8,128)(2,1)} custom-call(s32[6]{0:T(128)S(1)} %pad_add_fusion.4.refs_0_, bf16[384,1536]{1,0:T(8,128)(2,1)S(1)} %get-tuple-element.38.refs_1_, bf16[384,1536]{1,0:T(8,128)(2,1)} %collective-permute-done.24.refs_2_), custom_call_target="tpu_custom_call" | custom-call | flops 1024 | bytes 1024 | tf_op jit(solution)/shard_map/copied/pallas_call | solution.py:66
  206.8 2.9 %collective-permute-done.28.refs_2_ = bf16[64,1536]{1,0:T(8,128)(2,1)S(1)} collective-permute-done((bf16[64,1536]{1,0:T(8,128)(2,1)S(1)}, bf16[64,1536]{1,0:T(8,128)(2,1)S(1)}, u32[]{:S(2)}, u32[]{:S(2)}) %collective-permute-start.28) | collective-permute-done | bytes 196640 | tf_op jit(solution)/shard_map/ppermute | solution.py:36
  (101 shorter events, 44.4 us)
Async XLA Ops:
  7.2 69.5 %all-gather.2.cloned.1.call-start = ((), (), s32[]{:S(2)}) async-start(), calls=%async_computation.2 | async-start | bytes 1966080 | tf_op jit(solution)/shard_map/all_gather | solution.py:280
  7.2 18.7 %collective-permute-start.3 = (bf16[768,1536]{1,0:T(8,128)(2,1)}, bf16[768,1536]{1,0:T(8,128)(2,1)S(1)}, u32[]{:S(2)}, u32[]{:S(2)}) collective-permute-start(bf16[768,1536]{1,0:T(8,128)(2,1)} %refs_0_.1), channel_id=1, source_target_pairs={{0,32},{32,0},{2,34},{34,2},{4,36},{36,4},{6,38},{38,6},{1,33},{33... | collective-permute-start | bytes 7077896 | tf_op jit(solution)/shard_map/ppermute | solution.py:36
  10.5 11.2 %collective-permute-start = (bf16[64,1536]{1,0:T(8,128)(2,1)S(1)}, bf16[64,1536]{1,0:T(8,128)(2,1)S(1)}, u32[]{:S(2)}, u32[]{:S(2)}) collective-permute-start(bf16[64,1536]{1,0:T(8,128)(2,1)S(1)} %constant_dynamic-update-slice_fusion.refs_0_), channel_id=1, source_target_pairs={{0,65},{32,97},{2,67},{34,99},{4,69},{36,101},{6,71},{38,103},{1,0... | collective-permute-start | bytes 589832 | tf_op jit(solution)/shard_map/ppermute | solution.py:36
  13.3 8.4 %collective-permute-start.1 = (bf16[64,1536]{1,0:T(8,128)(2,1)S(1)}, bf16[64,1536]{1,0:T(8,128)(2,1)S(1)}, u32[]{:S(2)}, u32[]{:S(2)}) collective-permute-start(bf16[64,1536]{1,0:T(8,128)(2,1)S(1)} %constant_dynamic-update-slice_fusion.refs_0_), channel_id=1, source_target_pairs={{0,64},{32,96},{2,66},{34,98},{4,68},{36,100},{6,70},{38,102},{1,6... | collective-permute-start | bytes 589832 | tf_op jit(solution)/shard_map/ppermute | solution.py:36
  13.7 12.2 %collective-permute-start.2 = (bf16[64,1536]{1,0:T(8,128)(2,1)S(1)}, bf16[64,1536]{1,0:T(8,128)(2,1)S(1)}, u32[]{:S(2)}, u32[]{:S(2)}) collective-permute-start(bf16[64,1536]{1,0:T(8,128)(2,1)S(1)} %constant_dynamic-update-slice_fusion.refs_0_), channel_id=1, source_target_pairs={{0,1},{32,33},{2,3},{34,35},{4,5},{36,37},{6,7},{38,39},{1,64},{33... | collective-permute-start | bytes 589832 | tf_op jit(solution)/shard_map/ppermute | solution.py:36
  28.4 20.3 %collective-permute-start.4 = (bf16[128,1536]{1,0:T(8,128)(2,1)}, bf16[128,1536]{1,0:T(8,128)(2,1)}, u32[]{:S(2)}, u32[]{:S(2)}) collective-permute-start(bf16[128,1536]{1,0:T(8,128)(2,1)} %get-tuple-element.21.refs_0_), channel_id=1, source_target_pairs={{0,6},{32,38},{2,0},{34,32},{4,2},{36,34},{6,4},{38,36},{1,7},{33,... | collective-permute-start | bytes 1179656 | tf_op jit(solution)/shard_map/ppermute | solution.py:36
  32.2 16.6 %collective-permute-start.5 = (bf16[128,1536]{1,0:T(8,128)(2,1)}, bf16[128,1536]{1,0:T(8,128)(2,1)}, u32[]{:S(2)}, u32[]{:S(2)}) collective-permute-start(bf16[128,1536]{1,0:T(8,128)(2,1)} %get-tuple-element.21.refs_0_), channel_id=1, source_target_pairs={{0,4},{32,36},{2,6},{34,38},{4,0},{36,32},{6,2},{38,34},{1,5},{33,... | collective-permute-start | bytes 1179656 | tf_op jit(solution)/shard_map/ppermute | solution.py:36
  32.2 20.7 %collective-permute-start.6 = (bf16[128,1536]{1,0:T(8,128)(2,1)}, bf16[128,1536]{1,0:T(8,128)(2,1)}, u32[]{:S(2)}, u32[]{:S(2)}) collective-permute-start(bf16[128,1536]{1,0:T(8,128)(2,1)} %get-tuple-element.21.refs_0_), channel_id=1, source_target_pairs={{0,2},{32,34},{2,4},{34,36},{4,6},{36,38},{6,0},{38,32},{1,3},{33,... | collective-permute-start | bytes 1179656 | tf_op jit(solution)/shard_map/ppermute | solution.py:36
  35.7 29.1 %collective-permute-start.7 = (bf16[384,1536]{1,0:T(8,128)(2,1)}, bf16[384,1536]{1,0:T(8,128)(2,1)}, u32[]{:S(2)}, u32[]{:S(2)}) collective-permute-start(bf16[384,1536]{1,0:T(8,128)(2,1)} %get-tuple-element.23), channel_id=1, source_target_pairs={{0,64},{32,96},{2,66},{34,98},{4,68},{36,100},{6,70},{38,102},{1,6... | collective-permute-start | bytes 3538952 | tf_op jit(solution)/shard_map/ppermute | solution.py:36
  52.9 124.4 %reduce-scatter.3.cloned.1.call-start = ((), (), s32[]{:S(2)}) async-start(), calls=%async_computation.3 | async-start | bytes 1966080 | tf_op jit(solution)/shard_map/reduce_scatter | solution.py:306
  52.9 16.6 %collective-permute-start.8 = (bf16[384,1536]{1,0:T(8,128)(2,1)S(1)}, bf16[384,1536]{1,0:T(8,128)(2,1)}, u32[]{:S(2)}, u32[]{:S(2)}) collective-permute-start(bf16[384,1536]{1,0:T(8,128)(2,1)S(1)} %get-tuple-element.41.refs_0_), channel_id=1, source_target_pairs={{0,32},{32,0},{2,34},{34,2},{4,36},{36,4},{6,38},{38,6},{1,33},{33... | collective-permute-start | bytes 3538952 | tf_op jit(solution)/shard_map/ppermute | solution.py:36
  66.0 20.3 %collective-permute-start.15 = (bf16[128,1536]{1,0:T(8,128)(2,1)}, bf16[128,1536]{1,0:T(8,128)(2,1)}, u32[]{:S(2)}, u32[]{:S(2)}) collective-permute-start(bf16[128,1536]{1,0:T(8,128)(2,1)} %copy-done.4), channel_id=1, source_target_pairs={{0,24},{32,56},{2,26},{34,58},{4,28},{36,60},{6,30},{38,62},{1,25}... | collective-permute-start | bytes 1179656 | tf_op jit(solution)/shard_map/ppermute | solution.py:36
  68.5 18.5 %collective-permute-start.14 = (bf16[128,1536]{1,0:T(8,128)(2,1)S(1)}, bf16[128,1536]{1,0:T(8,128)(2,1)}, u32[]{:S(2)}, u32[]{:S(2)}) collective-permute-start(bf16[128,1536]{1,0:T(8,128)(2,1)S(1)} %get-tuple-element.27), channel_id=1, source_target_pairs={{0,16},{32,48},{2,18},{34,50},{4,20},{36,52},{6,22},{38,54},{1,17}... | collective-permute-start | bytes 1179656 | tf_op jit(solution)/shard_map/ppermute | solution.py:36
  69.0 20.6 %collective-permute-start.13 = (bf16[128,1536]{1,0:T(8,128)(2,1)S(1)}, bf16[128,1536]{1,0:T(8,128)(2,1)}, u32[]{:S(2)}, u32[]{:S(2)}) collective-permute-start(bf16[128,1536]{1,0:T(8,128)(2,1)S(1)} %get-tuple-element.26), channel_id=1, source_target_pairs={{0,8},{32,40},{2,10},{34,42},{4,12},{36,44},{6,14},{38,46},{1,9},{... | collective-permute-start | bytes 1179656 | tf_op jit(solution)/shard_map/ppermute | solution.py:36
  83.3 11.0 %collective-permute-start.12 = (bf16[128,1536]{1,0:T(8,128)(2,1)S(1)}, bf16[128,1536]{1,0:T(8,128)(2,1)S(1)}, u32[]{:S(2)}, u32[]{:S(2)}) collective-permute-start(bf16[128,1536]{1,0:T(8,128)(2,1)S(1)} %get-tuple-element.50), channel_id=1, source_target_pairs={{0,24},{32,56},{2,26},{34,58},{4,28},{36,60},{6,30},{38,62},{1,25}... | collective-permute-start | bytes 1179656 | tf_op jit(solution)/shard_map/ppermute | solution.py:36
  85.8 11.2 %collective-permute-start.11 = (bf16[128,1536]{1,0:T(8,128)(2,1)S(1)}, bf16[128,1536]{1,0:T(8,128)(2,1)S(1)}, u32[]{:S(2)}, u32[]{:S(2)}) collective-permute-start(bf16[128,1536]{1,0:T(8,128)(2,1)S(1)} %get-tuple-element.51), channel_id=1, source_target_pairs={{0,16},{32,48},{2,18},{34,50},{4,20},{36,52},{6,22},{38,54},{1,17}... | collective-permute-start | bytes 1179656 | tf_op jit(solution)/shard_map/ppermute | solution.py:36
  86.3 20.4 %collective-permute-start.10 = (bf16[128,1536]{1,0:T(8,128)(2,1)S(1)}, bf16[128,1536]{1,0:T(8,128)(2,1)S(1)}, u32[]{:S(2)}, u32[]{:S(2)}) collective-permute-start(bf16[128,1536]{1,0:T(8,128)(2,1)S(1)} %get-tuple-element.49), channel_id=1, source_target_pairs={{0,8},{32,40},{2,10},{34,42},{4,12},{36,44},{6,14},{38,46},{1,9},{... | collective-permute-start | bytes 1179656 | tf_op jit(solution)/shard_map/ppermute | solution.py:36
  109.0 10.3 %collective-permute-start.16 = (bf16[128,1536]{1,0:T(8,128)(2,1)S(1)}, bf16[128,1536]{1,0:T(8,128)(2,1)S(1)}, u32[]{:S(2)}, u32[]{:S(2)}) collective-permute-start(bf16[128,1536]{1,0:T(8,128)(2,1)S(1)} %get-tuple-element.37.refs_0_), channel_id=1, source_target_pairs={{0,24},{32,56},{2,26},{34,58},{4,28},{36,60},{6,30},{38,62},{1,25}... | collective-permute-start | bytes 1179656 | tf_op jit(solution)/shard_map/ppermute | solution.py:36
  109.1 11.2 %collective-permute-start.17 = (bf16[128,1536]{1,0:T(8,128)(2,1)S(1)}, bf16[128,1536]{1,0:T(8,128)(2,1)S(1)}, u32[]{:S(2)}, u32[]{:S(2)}) collective-permute-start(bf16[128,1536]{1,0:T(8,128)(2,1)S(1)} %get-tuple-element.37.refs_0_), channel_id=1, source_target_pairs={{0,16},{32,48},{2,18},{34,50},{4,20},{36,52},{6,22},{38,54},{1,17}... | collective-permute-start | bytes 1179656 | tf_op jit(solution)/shard_map/ppermute | solution.py:36
  109.7 20.4 %collective-permute-start.18 = (bf16[128,1536]{1,0:T(8,128)(2,1)S(1)}, bf16[128,1536]{1,0:T(8,128)(2,1)S(1)}, u32[]{:S(2)}, u32[]{:S(2)}) collective-permute-start(bf16[128,1536]{1,0:T(8,128)(2,1)S(1)} %get-tuple-element.37.refs_0_), channel_id=1, source_target_pairs={{0,8},{32,40},{2,10},{34,42},{4,12},{36,44},{6,14},{38,46},{1,9},{... | collective-permute-start | bytes 1179656 | tf_op jit(solution)/shard_map/ppermute | solution.py:36
  134.3 7.3 %collective-permute-start.19 = (bf16[768,1536]{1,0:T(8,128)(2,1)}, bf16[768,1536]{1,0:T(8,128)(2,1)}, u32[]{:S(2)}, u32[]{:S(2)}) collective-permute-start(bf16[768,1536]{1,0:T(8,128)(2,1)} %convolution_convert_fusion.1), channel_id=1, source_target_pairs={{0,32},{32,0},{2,34},{34,2},{4,36},{36,4},{6,38},{38,6},{1,33},{33... | collective-permute-start | bytes 7077896 | tf_op jit(solution)/shard_map/ppermute | solution.py:36
  138.6 73.0 %reduce-scatter.5.cloned.1.call-start = ((), (), s32[]{:S(2)}) async-start(), calls=%async_computation.4 | async-start | bytes 7077888 | tf_op jit(solution)/shard_map/reduce_scatter | solution.py:313
  138.6 10.9 %collective-permute-start.20 = (bf16[128,1536]{1,0:T(8,128)(2,1)S(1)}, bf16[128,1536]{1,0:T(8,128)(2,1)S(1)}, u32[]{:S(2)}, u32[]{:S(2)}) collective-permute-start(bf16[128,1536]{1,0:T(8,128)(2,1)S(1)} %get-tuple-element.30.refs_0_), channel_id=1, source_target_pairs={{0,24},{32,56},{2,26},{34,58},{4,28},{36,60},{6,30},{38,62},{1,25}... | collective-permute-start | bytes 1179656 | tf_op jit(solution)/shard_map/ppermute | solution.py:36
  139.5 11.9 %collective-permute-start.21 = (bf16[128,1536]{1,0:T(8,128)(2,1)S(1)}, bf16[128,1536]{1,0:T(8,128)(2,1)S(1)}, u32[]{:S(2)}, u32[]{:S(2)}) collective-permute-start(bf16[128,1536]{1,0:T(8,128)(2,1)S(1)} %get-tuple-element.30.refs_0_), channel_id=1, source_target_pairs={{0,16},{32,48},{2,18},{34,50},{4,20},{36,52},{6,22},{38,54},{1,17}... | collective-permute-start | bytes 1179656 | tf_op jit(solution)/shard_map/ppermute | solution.py:36
  139.6 21.0 %collective-permute-start.22 = (bf16[128,1536]{1,0:T(8,128)(2,1)S(1)}, bf16[128,1536]{1,0:T(8,128)(2,1)S(1)}, u32[]{:S(2)}, u32[]{:S(2)}) collective-permute-start(bf16[128,1536]{1,0:T(8,128)(2,1)S(1)} %get-tuple-element.30.refs_0_), channel_id=1, source_target_pairs={{0,8},{32,40},{2,10},{34,42},{4,12},{36,44},{6,14},{38,46},{1,9},{... | collective-permute-start | bytes 1179656 | tf_op jit(solution)/shard_map/ppermute | solution.py:36
  166.5 31.1 %collective-permute-start.24 = (bf16[384,1536]{1,0:T(8,128)(2,1)}, bf16[384,1536]{1,0:T(8,128)(2,1)}, u32[]{:S(2)}, u32[]{:S(2)}) collective-permute-start(bf16[384,1536]{1,0:T(8,128)(2,1)} %get-tuple-element.39), channel_id=1, source_target_pairs={{0,64},{32,96},{2,66},{34,98},{4,68},{36,100},{6,70},{38,102},{1,6... | collective-permute-start | bytes 3538952 | tf_op jit(solution)/shard_map/ppermute | solution.py:36
  175.5 22.1 %collective-permute-start.26 = (bf16[128,1536]{1,0:T(8,128)(2,1)S(1)}, bf16[128,1536]{1,0:T(8,128)(2,1)S(1)}, u32[]{:S(2)}, u32[]{:S(2)}) collective-permute-start(bf16[128,1536]{1,0:T(8,128)(2,1)S(1)} %get-tuple-element.43), channel_id=1, source_target_pairs={{0,6},{32,38},{2,0},{34,32},{4,2},{36,34},{6,4},{38,36},{1,7},{33,... | collective-permute-start | bytes 1179656 | tf_op jit(solution)/shard_map/ppermute | solution.py:36
  176.6 21.0 %collective-permute-start.25 = (bf16[128,1536]{1,0:T(8,128)(2,1)S(1)}, bf16[128,1536]{1,0:T(8,128)(2,1)S(1)}, u32[]{:S(2)}, u32[]{:S(2)}) collective-permute-start(bf16[128,1536]{1,0:T(8,128)(2,1)S(1)} %get-tuple-element.44), channel_id=1, source_target_pairs={{0,4},{32,36},{2,6},{34,38},{4,0},{36,32},{6,2},{38,34},{1,5},{33,... | collective-permute-start | bytes 1179656 | tf_op jit(solution)/shard_map/ppermute | solution.py:36
  177.3 20.3 %collective-permute-start.23 = (bf16[128,1536]{1,0:T(8,128)(2,1)S(1)}, bf16[128,1536]{1,0:T(8,128)(2,1)S(1)}, u32[]{:S(2)}, u32[]{:S(2)}) collective-permute-start(bf16[128,1536]{1,0:T(8,128)(2,1)S(1)} %get-tuple-element.42), channel_id=1, source_target_pairs={{0,2},{32,34},{2,4},{34,36},{4,6},{36,38},{6,0},{38,32},{1,3},{33,... | collective-permute-start | bytes 1179656 | tf_op jit(solution)/shard_map/ppermute | solution.py:36
  198.9 8.0 %collective-permute-start.27 = (bf16[64,1536]{1,0:T(8,128)(2,1)S(1)}, bf16[64,1536]{1,0:T(8,128)(2,1)S(1)}, u32[]{:S(2)}, u32[]{:S(2)}) collective-permute-start(bf16[64,1536]{1,0:T(8,128)(2,1)S(1)} %pad_maximum_fusion.1), channel_id=1, source_target_pairs={{0,1},{32,33},{2,3},{34,35},{4,5},{36,37},{6,7},{38,39},{1,64},{33... | collective-permute-start | bytes 589832 | tf_op jit(solution)/shard_map/ppermute | solution.py:36
  199.3 10.4 %collective-permute-start.28 = (bf16[64,1536]{1,0:T(8,128)(2,1)S(1)}, bf16[64,1536]{1,0:T(8,128)(2,1)S(1)}, u32[]{:S(2)}, u32[]{:S(2)}) collective-permute-start(bf16[64,1536]{1,0:T(8,128)(2,1)S(1)} %pad_maximum_fusion.2), channel_id=1, source_target_pairs={{0,64},{32,96},{2,66},{34,98},{4,68},{36,100},{6,70},{38,102},{1,6... | collective-permute-start | bytes 589832 | tf_op jit(solution)/shard_map/ppermute | solution.py:36
  201.2 9.6 %collective-permute-start.29 = (bf16[64,1536]{1,0:T(8,128)(2,1)S(1)}, bf16[64,1536]{1,0:T(8,128)(2,1)S(1)}, u32[]{:S(2)}, u32[]{:S(2)}) collective-permute-start(bf16[64,1536]{1,0:T(8,128)(2,1)S(1)} %pad_maximum_fusion.3), channel_id=1, source_target_pairs={{0,65},{32,97},{2,67},{34,99},{4,69},{36,101},{6,71},{38,103},{1,0... | collective-permute-start | bytes 589832 | tf_op jit(solution)/shard_map/ppermute | solution.py:36
  (14 other events, 32.6 us)
Sparse Core Ops, SparseCore 0:
  53.0 23.5 all-gather.1
  138.7 22.1 reduce-scatter.2
  166.5 13.3 reduce-scatter.4
